TPU v7x, 32 devices: a whole 2x2x4 slice. The times are simulated.
32 devices in a mesh: wide: 8 (over y, x, core), narrow: 4 (over z).
Axes of the slice: x: 2, y: 2, z: 4, core: 2. Of those that a mesh axis runs over, the one named last changes fastest.
Arguments:
- tokens: bfloat16 [2, 6304, 768], P(None, ('wide', 'narrow')), may hold values from -6 to 6
- page_mask: int32 [2, 6304], P(None, ('wide', 'narrow')), may hold values 0 or 1
- buckets: int32 [197, 197], replicated, may hold values from 0 to 731
- mask_token: float32 [768], replicated, may hold values from -6 to 6
- first_gain: float32 [768], replicated, may hold values from 0.5 to 1.5
- first_shift: float32 [768], replicated, may hold values from -3 to 3
- qkv_weight: bfloat16 [768, 3, 768], P(None, None, 'narrow'), may hold values from -0.21875 to 0.21875
- query_bias: float32 [768], P('narrow'), may hold values from -3 to 3
- value_bias: float32 [768], P('narrow'), may hold values from -3 to 3
- position_bias: float32 [12, 732], P('narrow'), may hold values from -4 to 4
- out_weight: bfloat16 [768, 768], P('narrow'), may hold values from -0.875 to 0.875
- out_bias: float32 [768], replicated, may hold values from -3 to 3
- attn_scale: float32 [768], replicated, may hold values from 0.5 to 2
- second_gain: float32 [768], replicated, may hold values from 0.5 to 1.5
- second_shift: float32 [768], replicated, may hold values from -3 to 3
- in_weight: bfloat16 [768, 3072], P(None, 'narrow'), may hold values from -0.21875 to 0.21875
- in_bias: float32 [3072], P('narrow'), may hold values from -3 to 3
- down_weight: bfloat16 [3072, 768], P('narrow'), may hold values from -0.109375 to 0.109375
- down_bias: float32 [768], replicated, may hold values from -3 to 3
- mlp_scale: float32 [768], replicated, may hold values from 0.5 to 2
- out_grad: bfloat16 [2, 6304, 768], P(None, ('wide', 'narrow')), may hold values from -6 to 6
Outputs:
- layer_out: bfloat16 [2, 6304, 768], P(None, ('wide', 'narrow'))
- tokens_grad: bfloat16 [2, 6304, 768], P(None, ('wide', 'narrow'))
- mask_token_grad: float32 [768], replicated
- first_gain_grad: float32 [768], replicated
- first_shift_grad: float32 [768], replicated
- qkv_weight_grad: float32 [768, 3, 768], P(None, None, 'narrow')
- query_bias_grad: float32 [768], P('narrow')
- value_bias_grad: float32 [768], P('narrow')
- position_bias_grad: float32 [12, 732], P('narrow')
- out_weight_grad: float32 [768, 768], P('narrow')
- out_bias_grad: float32 [768], replicated
- attn_scale_grad: float32 [768], replicated
- second_gain_grad: float32 [768], replicated
- second_shift_grad: float32 [768], replicated
- in_weight_grad: float32 [768, 3072], P(None, 'narrow')
- in_bias_grad: float32 [3072], P('narrow')
- down_weight_grad: float32 [3072, 768], P('narrow')
- down_bias_grad: float32 [768], replicated
- mlp_scale_grad: float32 [768], replicated
All inputs are finite; a program needn't handle non-finite values. No bound on the sum of `page_mask` on one device may be relied on, other than what follows from the above.
Results may differ from a plain program's by a relative error of at most 0.015.
Values may be sent and summed in bfloat16 or wider, within the bound.
No kernel may reach another device: no remote copies, remote signals or barrier semaphores. Data moves between devices by JAX's collectives and lax.ppermute only.
A program may use at most 128 MiB of HBM per device.

v0:
```python
import jax
import jax.numpy as jnp
from jax import lax
from jax.sharding import PartitionSpec as P

SEQ = 197


EPSILON = 1e-06
ROOT_HALF = 0.7071067811865476
DENSITY = 0.3989422804014327


def layer_norm(values, gain, shift):
    center = values - jnp.mean(values, axis=-1, keepdims=True)
    spread = jnp.mean(center * center, axis=-1, keepdims=True)
    inverse = lax.rsqrt(spread + EPSILON)
    normed = center * inverse
    return (normed * gain + shift, normed, inverse)


def norm_back(grad_out, normed, inverse, gain):
    scaled = grad_out * gain
    inner_mean = jnp.mean(scaled, axis=-1, keepdims=True)
    cross_mean = jnp.mean(scaled * normed, axis=-1, keepdims=True)
    return inverse * (scaled - inner_mean - normed * cross_mean)


def gelu_slope(values):
    return 0.5 * (1.0 + lax.erf(values * ROOT_HALF)) + values * DENSITY * jnp.exp(
        -0.5 * values * values
    )


def column_sum(values):
    return jnp.sum(values, axis=0, dtype=jnp.float32)


def split_three(values):
    upper = values.astype(jnp.bfloat16)
    rest = values - upper.astype(jnp.float32)
    middle_part = rest.astype(jnp.bfloat16)
    lower = (rest - middle_part.astype(jnp.float32)).astype(jnp.bfloat16)
    return jnp.concatenate([upper, middle_part, lower], axis=0)


def body(
    tokens,
    page_mask,
    buckets,
    mask_token,
    first_gain,
    first_shift,
    qkv_weight,
    query_bias,
    value_bias,
    position_bias,
    out_weight,
    out_bias,
    attn_scale,
    second_gain,
    second_shift,
    in_weight,
    in_bias,
    down_weight,
    down_bias,
    mlp_scale,
    out_grad,
):
    micro_count, local_rows, model_width = tokens.shape
    group_rows = local_rows * lax.axis_size("narrow")
    page_count = group_rows // SEQ
    local_heads = position_bias.shape[0]
    bucket_count = position_bias.shape[1]
    local_width = qkv_weight.shape[2]
    head_size = local_width // local_heads
    factor = head_size ** (-0.5)
    head_shape = (page_count, SEQ, local_heads, head_size)
    qkv_flat = qkv_weight.reshape(model_width, 3 * local_width)
    qkv_shift = jnp.concatenate([query_bias, jnp.zeros_like(query_bias), value_bias])
    bucket_table = (
        buckets.reshape(-1)[:, None] == jnp.arange(bucket_count, dtype=jnp.int32)[None, :]
    ).astype(jnp.bfloat16)
    bias_parts = jnp.einsum(
        "kb,nb->kn", split_three(position_bias), bucket_table, preferred_element_type=jnp.float32
    )
    bias_grid = (
        bias_parts[:local_heads]
        + bias_parts[local_heads : 2 * local_heads]
        + bias_parts[2 * local_heads :]
    ).reshape(local_heads, SEQ, SEQ)
    not_class = jnp.arange(local_rows, dtype=jnp.int32) % SEQ != 0

    def project_qkv(shard_rows):
        return (
            jnp.dot(shard_rows, qkv_flat, preferred_element_type=jnp.float32) + qkv_shift
        ).astype(jnp.bfloat16)

    def project_in(shard_rows):
        return jnp.dot(shard_rows, in_weight, preferred_element_type=jnp.float32) + in_bias

    def split_qkv(qkv_rows):
        queries = qkv_rows[:, :local_width].reshape(head_shape)
        keys_all = qkv_rows[:, local_width : 2 * local_width].reshape(head_shape)
        values_all = qkv_rows[:, 2 * local_width :].reshape(head_shape)
        scores = (
            jnp.einsum("pqhe,pkhe->phqk", queries, keys_all, preferred_element_type=jnp.float32)
            * factor
            + bias_grid[None]
        )
        return (queries, keys_all, values_all, scores)

    def weigh(probs_low, values_all):
        mixed_rows = jnp.einsum(
            "phqk,pkhe->pqhe", probs_low, values_all, preferred_element_type=jnp.float32
        )
        return mixed_rows.astype(jnp.bfloat16).reshape(group_rows, local_width)

    outputs = []
    stored = []
    for index in range(micro_count):
        masked_rows = (page_mask[index] > 0) & not_class
        masked_in = jnp.where(
            masked_rows[:, None], mask_token[None, :], tokens[index].astype(jnp.float32)
        )
        first_out, first_normed, first_inverse = layer_norm(masked_in, first_gain, first_shift)
        first_low = first_out.astype(jnp.bfloat16)
        first_full = lax.all_gather(first_low, "narrow", axis=0, tiled=True)
        queries, keys_all, values_all, scores = split_qkv(project_qkv(first_full))
        row_top = jnp.max(scores, axis=-1, keepdims=True)
        exponent = jnp.exp(scores - row_top)
        row_total = jnp.sum(exponent, axis=-1, keepdims=True)
        log_total = row_top + jnp.log(row_total)
        mixed_rows = weigh((exponent / row_total).astype(jnp.bfloat16), values_all)
        attn_out = (
            lax.psum_scatter(
                jnp.dot(mixed_rows, out_weight, preferred_element_type=jnp.float32),
                "narrow",
                scatter_dimension=0,
                tiled=True,
            )
            + out_bias
        )
        middle = masked_in + attn_scale * attn_out
        second_out, second_normed, second_inverse = layer_norm(middle, second_gain, second_shift)
        second_low = second_out.astype(jnp.bfloat16)
        second_full = lax.all_gather(second_low, "narrow", axis=0, tiled=True)
        hidden = jax.nn.gelu(project_in(second_full), approximate=False).astype(jnp.bfloat16)
        mlp_out = (
            lax.psum_scatter(
                jnp.dot(hidden, down_weight, preferred_element_type=jnp.float32).astype(
                    jnp.bfloat16
                ),
                "narrow",
                scatter_dimension=0,
                tiled=True,
            ).astype(jnp.float32)
            + down_bias
        )
        outputs.append((middle + mlp_scale * mlp_out).astype(jnp.bfloat16))
        kept_first, kept_second = (first_full, second_full)
        stored.append(
            (
                masked_rows,
                first_low,
                first_normed,
                first_inverse,
                log_total,
                attn_out,
                second_low,
                second_normed,
                second_inverse,
                mlp_out,
                kept_first,
                kept_second,
            )
        )
    grads_in = [None] * micro_count
    weight_total = None
    small_total = None
    for index in reversed(range(micro_count)):
        (
            masked_rows,
            first_low,
            first_normed,
            first_inverse,
            log_total,
            attn_out,
            second_low,
            second_normed,
            second_inverse,
            mlp_out,
            kept_first,
            kept_second,
        ) = stored[index]
        grad_out = out_grad[index].astype(jnp.float32)
        mlp_grad = (grad_out * mlp_scale).astype(jnp.bfloat16)
        mlp_grad_full = lax.all_gather(mlp_grad, "narrow", axis=0, tiled=True)
        hidden_pre = project_in(kept_second)
        hidden_again = jax.nn.gelu(hidden_pre, approximate=False).astype(jnp.bfloat16)
        down_w_grad = jnp.einsum(
            "rf,rd->fd", hidden_again, mlp_grad_full, preferred_element_type=jnp.float32
        )
        hidden_grad = jnp.einsum(
            "rd,fd->rf", mlp_grad_full, down_weight, preferred_element_type=jnp.float32
        )
        pre_grad = (hidden_grad * gelu_slope(hidden_pre)).astype(jnp.bfloat16)
        in_b_grad = column_sum(pre_grad)
        in_w_grad = jnp.einsum(
            "rd,rf->df", kept_second, pre_grad, preferred_element_type=jnp.float32
        )
        second_grad = lax.psum_scatter(
            jnp.einsum("rf,df->rd", pre_grad, in_weight, preferred_element_type=jnp.float32),
            "narrow",
            scatter_dimension=0,
            tiled=True,
        )
        middle_grad = grad_out + norm_back(second_grad, second_normed, second_inverse, second_gain)
        attn_grad = (middle_grad * attn_scale).astype(jnp.bfloat16)
        attn_grad_full = lax.all_gather(attn_grad, "narrow", axis=0, tiled=True)
        queries, keys_all, values_all, scores = split_qkv(project_qkv(kept_first))
        attention = jnp.exp(scores - log_total)
        probs_low = attention.astype(jnp.bfloat16)
        mixed_rows = weigh(probs_low, values_all)
        out_w_grad = jnp.einsum(
            "rc,rd->cd", mixed_rows, attn_grad_full, preferred_element_type=jnp.float32
        )
        mixed_grad = (
            jnp.einsum("rd,cd->rc", attn_grad_full, out_weight, preferred_element_type=jnp.float32)
            .astype(jnp.bfloat16)
            .reshape(head_shape)
        )
        values_grad = jnp.einsum(
            "phqk,pqhe->pkhe", probs_low, mixed_grad, preferred_element_type=jnp.float32
        ).astype(jnp.bfloat16)
        probs_grad = jnp.einsum(
            "pqhe,pkhe->phqk", mixed_grad, values_all, preferred_element_type=jnp.float32
        )
        score_grad = (
            attention * (probs_grad - jnp.sum(attention * probs_grad, axis=-1, keepdims=True))
        ).astype(jnp.bfloat16)
        queries_grad = (
            jnp.einsum("phqk,pkhe->pqhe", score_grad, keys_all, preferred_element_type=jnp.float32)
            * factor
        ).astype(jnp.bfloat16)
        keys_grad = (
            jnp.einsum("phqk,pqhe->pkhe", score_grad, queries, preferred_element_type=jnp.float32)
            * factor
        ).astype(jnp.bfloat16)
        grid_grad = jnp.sum(score_grad, axis=0, dtype=jnp.float32).reshape(local_heads, SEQ * SEQ)
        table_parts = jnp.einsum(
            "kn,nb->kb", split_three(grid_grad), bucket_table, preferred_element_type=jnp.float32
        )
        table_grad = (
            table_parts[:local_heads]
            + table_parts[local_heads : 2 * local_heads]
            + table_parts[2 * local_heads :]
        )
        qkv_grad = jnp.concatenate(
            [
                queries_grad.reshape(group_rows, local_width),
                keys_grad.reshape(group_rows, local_width),
                values_grad.reshape(group_rows, local_width),
            ],
            axis=1,
        )
        query_b_grad = column_sum(qkv_grad[:, :local_width])
        value_b_grad = column_sum(qkv_grad[:, 2 * local_width :])
        qkv_w_grad = jnp.einsum(
            "rd,rc->dc", kept_first, qkv_grad, preferred_element_type=jnp.float32
        ).reshape(model_width, 3, local_width)
        first_grad = lax.psum_scatter(
            jnp.einsum("rc,dc->rd", qkv_grad, qkv_flat, preferred_element_type=jnp.float32),
            "narrow",
            scatter_dimension=0,
            tiled=True,
        )
        in_grad = middle_grad + norm_back(first_grad, first_normed, first_inverse, first_gain)
        grads_in[index] = jnp.where(masked_rows[:, None], 0.0, in_grad).astype(jnp.bfloat16)
        micro_small = (
            jnp.sum(jnp.where(masked_rows[:, None], in_grad, 0.0), axis=0),
            jnp.sum(first_grad * first_normed, axis=0),
            jnp.sum(first_grad, axis=0),
            jnp.sum(middle_grad * attn_scale, axis=0),
            jnp.sum(middle_grad * attn_out, axis=0),
            jnp.sum(second_grad * second_normed, axis=0),
            jnp.sum(second_grad, axis=0),
            jnp.sum(grad_out * mlp_scale, axis=0),
            jnp.sum(grad_out * mlp_out, axis=0),
        )
        micro_grads = (
            qkv_w_grad,
            query_b_grad,
            value_b_grad,
            table_grad,
            out_w_grad,
            in_w_grad,
            in_b_grad,
            down_w_grad,
        )
        weight_total = (
            micro_grads
            if weight_total is None
            else jax.tree.map(jnp.add, weight_total, micro_grads)
        )
        small_total = (
            micro_small if small_total is None else jax.tree.map(jnp.add, small_total, micro_small)
        )
    weight_total = lax.psum(
        (
            weight_total[0],
            weight_total[1],
            weight_total[2],
            weight_total[3],
            weight_total[4],
            weight_total[5],
            weight_total[6],
            weight_total[7],
        ),
        "wide",
    )
    small_total = lax.psum(
        (
            small_total[0],
            small_total[1],
            small_total[2],
            small_total[3],
            small_total[4],
            small_total[5],
            small_total[6],
            small_total[7],
            small_total[8],
        ),
        ("wide", "narrow"),
    )
    return (
        jnp.stack(outputs),
        jnp.stack(grads_in),
        small_total[0],
        small_total[1],
        small_total[2],
        weight_total[0],
        weight_total[1],
        weight_total[2],
        weight_total[3],
        weight_total[4],
        small_total[3],
        small_total[4],
        small_total[5],
        small_total[6],
        weight_total[5],
        weight_total[6],
        weight_total[7],
        small_total[7],
        small_total[8],
    )


def solution(mesh):
    placed = (
        P(None, ("wide", "narrow"), None),
        P(None, ("wide", "narrow")),
        P(),
        P(),
        P(),
        P(),
        P(None, None, "narrow"),
        P("narrow"),
        P("narrow"),
        P("narrow", None),
        P("narrow", None),
        P(),
        P(),
        P(),
        P(),
        P(None, "narrow"),
        P("narrow"),
        P("narrow", None),
        P(),
        P(),
        P(None, ("wide", "narrow"), None),
    )
    return jax.shard_map(
        body,
        mesh=mesh,
        in_specs=placed,
        out_specs=(
            P(None, ("wide", "narrow"), None),
            P(None, ("wide", "narrow"), None),
            P(),
            P(),
            P(),
            P(None, None, "narrow"),
            P("narrow"),
            P("narrow"),
            P("narrow", None),
            P("narrow", None),
            P(),
            P(),
            P(),
            P(),
            P(None, "narrow"),
            P("narrow"),
            P("narrow", None),
            P(),
            P(),
        ),
        check_vma=False,
    )
```

profile of v0, /device:TPU:0, one launch (start us, length us, event | category | flops | bytes accessed | tf_op | source)
XLA Modules:
  0.0 875.8 jit_solution(6687401247204999386)
XLA Ops:
  14.1 19.6 %fusion.10 = f32[9,38809]{1,0:T(8,128)S(1)} fusion(s32[38809]{0:T(1024)S(1)} %eq.17, bf16[3,732]{1,0:T(4,128)(2,1)S(1)} %get-tuple-element.230, bf16[3,732]{1,0:T(4,128)(2,1)S(1)} %get-tuple-element.231, bf16[3,732]{1,0:T(4,128)(2,1)S(1)} %get-tuple-element.229), kind=kOutput, calls=%fused_computation.3 | convolution fusion | flops 539795136 | bytes 1565536 | tf_op jit(solution)/shard_map/kb,nb->kn/dot_general | solution.py:84
  36.9 9.9 %all-gather.21.cloned.1.call-done = bf16[4,197,768]{2,1,0:T(8,128)(2,1)} async-done(((bf16[1,197,768]{2,1,0:T(8,128)(2,1)}), bf16[4,197,768]{2,1,0:T(8,128)(2,1)}) %all-gather.21.cloned.1.call-update) | async-done | bytes 1210384 | tf_op jit(solution)/shard_map/all_gather | solution.py:128
  49.5 2.7 add_convert_fusion
  63.5 15.9 %all-gather.17.cloned.1.call-done = bf16[4,197,768]{2,1,0:T(8,128)(2,1)} async-done(((bf16[1,197,768]{2,1,0:T(8,128)(2,1)}), bf16[4,197,768]{2,1,0:T(8,128)(2,1)}) %all-gather.17.cloned.1.call-update) | async-done | bytes 1210384 | tf_op jit(solution)/shard_map/all_gather | solution.py:128
  79.4 2.7 reshape.287
  82.1 2.7 add_convert_fusion.1
  107.5 3.1 fusion.167
  112.6 86.0 %fusion.150 = (f32[200,768]{1,0:T(8,128)S(1)}, f32[200,768]{1,0:T(8,128)S(1)}) fusion(f32[788,768]{1,0:T(8,128)} %fusion.168, f32[788,768]{1,0:T(8,128)} %fusion.167), kind=kCustom, calls=%all-reduce-scatter.10 | all-reduce-scatter fusion | flops 1228801 | bytes 6070784
  199.2 3.4 collective-permute-start
  205.9 3.7 concatenate.24
  209.6 3.7 concatenate.26
  217.7 28.5 %all-gather.23.cloned.1.call-done = bf16[4,197,768]{2,1,0:T(8,128)(2,1)} async-done(((bf16[1,197,768]{2,1,0:T(8,128)(2,1)}), bf16[4,197,768]{2,1,0:T(8,128)(2,1)}) %all-gather.23.cloned.1.call-update) | async-done | bytes 1210384 | tf_op jit(solution)/shard_map/all_gather | solution.py:147
  248.9 3.9 fusion.169
  252.8 25.8 %all-gather.19.cloned.1.call-done = bf16[4,197,768]{2,1,0:T(8,128)(2,1)} async-done(((bf16[1,197,768]{2,1,0:T(8,128)(2,1)}), bf16[4,197,768]{2,1,0:T(8,128)(2,1)}) %all-gather.19.cloned.1.call-update) | async-done | bytes 1210384 | tf_op jit(solution)/shard_map/all_gather | solution.py:147
  281.2 13.7 %fusion.16 = (bf16[788,768]{1,0:T(8,128)(2,1)S(1)}, bf16[788,768]{1,0:T(8,128)(2,1)S(1)}, f32[788,768]{1,0:T(8,128)}) fusion(f32[768]{0:T(1024)S(1)} %copy-done.98, f32[788,768]{1,0:T(8,128)} %fusion.169, bf16[788,768]{1,0:T(8,128)(2,1)} %reshape.289, bf16[768,768]{1,0:T(8,128)(2,1)S(1)} %copy-done), kind=kOutput, calls=%fused_computation.27 | convolution fusion | flops 1009446912 | bytes 9655296 | tf_op jit(solution)/shard_map/dot_general | solution.py:100
  299.3 46.7 %fusion.151 = (bf16[200,768]{1,0:T(8,128)(2,1)}, bf16[200,768]{1,0:T(8,128)(2,1)}) fusion(bf16[788,768]{1,0:T(8,128)(2,1)} %convolution_convert_fusion, bf16[788,768]{1,0:T(8,128)(2,1)} %convolution_convert_fusion.1), kind=kCustom, calls=%all-reduce-scatter.11 | all-reduce-scatter fusion | flops 1228801 | bytes 3035648
  347.4 3.0 collective-permute-start.1
  354.5 4.0 concatenate.25
  358.5 4.0 concatenate.27
  366.3 3.0 fusion.66
  369.3 25.7 %all-gather.29.cloned.1.call-done = bf16[4,197,768]{2,1,0:T(8,128)(2,1)} async-done(((bf16[1,197,768]{2,1,0:T(8,128)(2,1)}), bf16[4,197,768]{2,1,0:T(8,128)(2,1)}) %all-gather.29.cloned.1.call-update) | async-done | bytes 1210384 | tf_op jit(solution)/shard_map/all_gather | solution.py:198
  397.7 5.7 convert_reduce_fusion.3
  403.4 24.1 %all-gather.25.cloned.1.call-done = bf16[4,197,768]{2,1,0:T(8,128)(2,1)} async-done(((bf16[1,197,768]{2,1,0:T(8,128)(2,1)}), bf16[4,197,768]{2,1,0:T(8,128)(2,1)}) %all-gather.25.cloned.1.call-update) | async-done | bytes 1210384 | tf_op jit(solution)/shard_map/all_gather | solution.py:198
  427.5 2.7 reshape.295
  430.1 4.7 convert_reduce_fusion.2
  434.8 2.7 fusion.170
  437.5 2.6 fusion.172
  440.1 85.9 %fusion.149 = (f32[200,768]{1,0:T(8,128)S(1)}, f32[200,768]{1,0:T(8,128)S(1)}) fusion(f32[788,768]{1,0:T(8,128)} %fusion.172, f32[788,768]{1,0:T(8,128)} %fusion.170), kind=kCustom, calls=%all-reduce-scatter.9 | all-reduce-scatter fusion | flops 1228801 | bytes 6070784
  526.1 3.0 collective-permute-start.4
  535.6 3.1 multiply_reduce_fusion.2
  538.8 2.7 multiply_reduce_fusion.5
  547.8 3.4 fusion.177
  552.8 2.9 convolution_add_fusion
  555.8 2.9 convolution_add_fusion.1
  560.5 12.9 %all-gather.27.cloned.1.call-done = bf16[4,197,768]{2,1,0:T(8,128)(2,1)} async-done(((bf16[1,197,768]{2,1,0:T(8,128)(2,1)}), bf16[4,197,768]{2,1,0:T(8,128)(2,1)}) %all-gather.27.cloned.1.call-update) | async-done | bytes 1210384 | tf_op jit(solution)/shard_map/all_gather | solution.py:220
  586.5 18.8 %all-gather.31.cloned.1.call-done = bf16[4,197,768]{2,1,0:T(8,128)(2,1)} async-done(((bf16[1,197,768]{2,1,0:T(8,128)(2,1)}), bf16[4,197,768]{2,1,0:T(8,128)(2,1)}) %all-gather.31.cloned.1.call-update) | async-done | bytes 1210384 | tf_op jit(solution)/shard_map/all_gather | solution.py:220
  605.4 2.7 reshape.301
  617.9 3.7 fusion.174
  639.5 4.0 fusion.171
  645.8 86.7 %fusion.148 = (f32[200,768]{1,0:T(8,128)S(1)}, f32[200,768]{1,0:T(8,128)}) fusion(f32[788,768]{1,0:T(8,128)} %fusion.173, f32[788,768]{1,0:T(8,128)} %fusion.171), kind=kCustom, calls=%all-reduce-scatter.8 | all-reduce-scatter fusion | flops 1228801 | bytes 6070784
  733.4 2.9 collective-permute-start.5
  741.8 21.7 %fusion.8 = f32[9,732]{1,0:T(8,128)S(1)} fusion(s32[38809]{0:T(1024)S(1)} %copy-done.62, bf16[3,38809]{1,0:T(4,128)(2,1)S(1)} %copy-done.53, bf16[3,38809]{1,0:T(4,128)(2,1)S(1)} %copy-done.54, bf16[3,38809]{1,0:T(4,128)(2,1)S(1)} %copy-done.52), kind=kOutput, calls=%fused_computation.1 | convolution fusion | flops 541851264 | bytes 880150 | tf_op jit(solution)/shard_map/kn,nb->kb/dot_general | solution.py:251
  763.5 22.0 %fusion.9 = f32[9,732]{1,0:T(8,128)S(1)} fusion(s32[38809]{0:T(1024)S(1)} %copy-done.62, bf16[3,38809]{1,0:T(4,128)(2,1)S(1)} %copy-done.56, bf16[3,38809]{1,0:T(4,128)(2,1)S(1)} %copy-done.57, bf16[3,38809]{1,0:T(4,128)(2,1)S(1)} %copy-done.55), kind=kOutput, calls=%fused_computation.2 | convolution fusion | flops 541851264 | bytes 880150 | tf_op jit(solution)/shard_map/kn,nb->kb/dot_general | solution.py:251
  785.8 23.6 %all-reduce.17 = (f32[192]{0:T(256)}, f32[192]{0:T(256)}, f32[3,732]{1,0:T(4,128)}, f32[768]{0:T(1024)}) all-reduce(f32[192]{0:T(256)S(1)} %add.390, f32[192]{0:T(256)S(1)} %add.392, f32[3,732]{1,0:T(4,128)S(1)} %fusion.141, f32[768]{0:T(1024)S(1)} %add.404), channel_id=1, replica_groups=mesh['wide'=8,'narrow'=4] {'wide'}, use_global_device_ids=true, to_apply=%region_42.43 | all-reduce | flops 3348 | bytes 26784 | tf_op jit(solution)/shard_map/psum | solution.py:309
  809.4 3.5 concatenate.29
  812.9 2.9 concatenate.31
  821.5 39.8 %all-reduce.16 = (f32[768]{0:T(1024)}, f32[768]{0:T(1024)}, f32[768]{0:T(1024)}, f32[768]{0:T(1024)}, f32[768]{0:T(1024)}, /*index=5*/f32[768]{0:T(1024)}, f32[768]{0:T(1024)}, f32[768]{0:T(1024)}, f32[768]{0:T(1024)}) all-reduce(f32[768]{0:T(1024)S(1)} %add.384, ...), channel_id=1, replica_groups=mesh['wide'=8,'narrow'=4] {'wide','narrow'}, use_global_device_ids=true, to_apply=%region_32.33 | all-reduce | flops 6912 | bytes 55296 | tf_op jit(solution)/shard_map/psum | solution.py:322
  861.4 2.9 copy.341
  (404 shorter events, 153.5 us)
Async XLA Ops:
  7.2 241.7 %copy-start = (bf16[768,768]{1,0:T(8,128)(2,1)S(1)}, bf16[768,768]{1,0:T(8,128)(2,1)}, u32[]{:S(2)}) copy-start(bf16[768,768]{1,0:T(8,128)(2,1)} %param.36) | copy-start | bytes 3538948
  7.2 39.6 %all-gather.21.cloned.1.call-start = ((), (), s32[]{:S(2)}) async-start(), calls=%async_computation.2 | async-start | bytes 1536000 | tf_op jit(solution)/shard_map/all_gather | solution.py:128
  10.4 202.8 %copy-start.69 = (pred[197]{0:T(512)(128)(4,1)}, pred[197]{0:T(512)(128)(4,1)S(1)}, u32[]{:S(2)}) copy-start(pred[197]{0:T(512)(128)(4,1)S(1)} %get-tuple-element.263) | copy-start | bytes 595
  10.4 202.8 %copy-start.71 = (pred[197]{0:T(512)(128)(4,1)}, pred[197]{0:T(512)(128)(4,1)S(1)}, u32[]{:S(2)}) copy-start(pred[197]{0:T(512)(128)(4,1)S(1)} %get-tuple-element.264) | copy-start | bytes 595
  10.7 202.6 %copy-start.6 = (bf16[197,768]{1,0:T(8,128)(2,1)}, bf16[197,768]{1,0:T(8,128)(2,1)S(1)}, u32[]{:S(2)}) copy-start(bf16[197,768]{1,0:T(8,128)(2,1)S(1)} %get-tuple-element.201) | copy-start | bytes 907780
  11.1 202.2 %copy-start.8 = (bf16[197,768]{1,0:T(8,128)(2,1)}, bf16[197,768]{1,0:T(8,128)(2,1)S(1)}, u32[]{:S(2)}) copy-start(bf16[197,768]{1,0:T(8,128)(2,1)S(1)} %get-tuple-element.199) | copy-start | bytes 907780
  12.7 66.7 %all-gather.17.cloned.1.call-start = ((), (), s32[]{:S(2)}) async-start(), calls=%async_computation | async-start | bytes 1536000 | tf_op jit(solution)/shard_map/all_gather | solution.py:128
  13.5 232.7 %all-gather.23.cloned.1.call-start = ((), (), s32[]{:S(2)}) async-start(), calls=%async_computation.3 | async-start | bytes 1536000 | tf_op jit(solution)/shard_map/all_gather | solution.py:147
  14.1 19.6 %copy-start.61 = (s32[38809]{0:T(1024)}, s32[38809]{0:T(1024)S(1)}, u32[]{:S(2)}) copy-start(s32[38809]{0:T(1024)S(1)} %eq.17) | copy-start | bytes 465712
  112.6 92.1 %copy-start.94 = (u32[32]{0:T(128)S(1)}, u32[32]{0:T(128)}, u32[]{:S(2)}) copy-start(u32[32]{0:T(128)} %constant.110) | copy-start | bytes 388
  199.2 6.6 collective-permute-start
  202.7 6.9 collective-permute-start.2
  215.3 33.6 %copy-start.83 = (f32[197]{0:T(256)}, f32[197]{0:T(256)S(1)}, u32[]{:S(2)}) copy-start(f32[197]{0:T(256)S(1)} %add_rsqrt_fusion) | copy-start | bytes 2368
  215.5 33.3 %copy-start.85 = (f32[197]{0:T(256)}, f32[197]{0:T(256)S(1)}, u32[]{:S(2)}) copy-start(f32[197]{0:T(256)S(1)} %add_rsqrt_fusion.2) | copy-start | bytes 2368
  216.7 61.9 %all-gather.19.cloned.1.call-start = ((), (), s32[]{:S(2)}) async-start(), calls=%async_computation.1 | async-start | bytes 1536000 | tf_op jit(solution)/shard_map/all_gather | solution.py:147
  217.2 177.8 %all-gather.29.cloned.1.call-start = ((), (), s32[]{:S(2)}) async-start(), calls=%async_computation.6 | async-start | bytes 1536000 | tf_op jit(solution)/shard_map/all_gather | solution.py:198
  252.8 28.5 %copy-start.98 = (f32[768]{0:T(1024)S(1)}, f32[768]{0:T(1024)}, u32[]{:S(2)}) copy-start(f32[768]{0:T(1024)} %param.37) | copy-start | bytes 9220
  299.3 53.4 %copy-start.32 = (bf16[2,197,768]{2,0,1:T(2,128)(2,1)S(1)}, bf16[2,197,768]{2,0,1:T(2,128)(2,1)}, u32[]{:S(2)}) copy-start(bf16[2,197,768]{2,0,1:T(2,128)(2,1)} %param.41) | copy-start | bytes 1815556
  345.9 16.6 %copy-start.64 = (f32[768]{0:T(1024)S(1)}, f32[768]{0:T(1024)}, u32[]{:S(2)}) copy-start(f32[768]{0:T(1024)} %param.40) | copy-start | bytes 9220
  345.9 16.6 %copy-start.77 = (f32[768]{0:T(1024)S(1)}, f32[768]{0:T(1024)}, u32[]{:S(2)}) copy-start(f32[768]{0:T(1024)} %param.39) | copy-start | bytes 9220
  347.4 7.1 collective-permute-start.1
  350.4 8.1 collective-permute-start.3
  365.5 62.0 %all-gather.25.cloned.1.call-start = ((), (), s32[]{:S(2)}) async-start(), calls=%async_computation.4 | async-start | bytes 1536000 | tf_op jit(solution)/shard_map/all_gather | solution.py:198
  366.1 207.4 %all-gather.27.cloned.1.call-start = ((), (), s32[]{:S(2)}) async-start(), calls=%async_computation.5 | async-start | bytes 1536000 | tf_op jit(solution)/shard_map/all_gather | solution.py:220
  366.3 31.4 %copy-start.99 = (f32[768]{0:T(1024)S(1)}, f32[768]{0:T(1024)}, u32[]{:S(2)}) copy-start(f32[768]{0:T(1024)} %param.37) | copy-start | bytes 9220
  526.1 4.9 collective-permute-start.4
  529.1 4.1 collective-permute-start.6
  542.5 62.9 %all-gather.31.cloned.1.call-start = ((), (), s32[]{:S(2)}) async-start(), calls=%async_computation.7 | async-start | bytes 1536000 | tf_op jit(solution)/shard_map/all_gather | solution.py:220
  560.1 301.3 %all-reduce.25.cloned.1.call-start = ((), (), s32[]{:S(2)}) async-start(), calls=%async_computation.8 | async-start | bytes 14155776 | tf_op jit(solution)/shard_map/psum | solution.py:309
  585.2 22.8 %copy-start.50 = (bf16[192,768]{1,0:T(8,128)(2,1)S(1)}, bf16[192,768]{1,0:T(8,128)(2,1)}, u32[]{:S(2)}) copy-start(bf16[192,768]{1,0:T(8,128)(2,1)} %param.31) | copy-start | bytes 884740
  645.8 92.3 %copy-start.41 = (bf16[788,192]{0,1:T(8,128)(2,1)S(1)}, bf16[788,192]{0,1:T(8,128)(2,1)}, u32[]{:S(2)}) copy-start(bf16[788,192]{0,1:T(8,128)(2,1)} %reshape.281) | copy-start | bytes 907780
  733.4 76.0 %collective-permute-start.5 = (f32[9,768]{1,0:T(8,128)S(1)}, f32[9,768]{1,0:T(8,128)S(1)}, u32[]{:S(2)}, u32[]{:S(2)}) collective-permute-start(f32[9,768]{1,0:T(8,128)S(1)} %slice.110), channel_id=1, source_target_pairs={{0,1},{1,2},{2,3},{4,5},{5,6},{6,7},{8,9},{9,10},{10,11},{12,13},{... | collective-permute-start | bytes 82952
  736.2 76.6 %collective-permute-start.7 = (f32[9,768]{1,0:T(8,128)S(1)}, f32[9,768]{1,0:T(8,128)S(1)}, u32[]{:S(2)}, u32[]{:S(2)}) collective-permute-start(f32[9,768]{1,0:T(8,128)S(1)} %slice.112), channel_id=1, source_target_pairs={{0,1},{1,2},{2,3},{4,5},{5,6},{6,7},{8,9},{9,10},{10,11},{12,13},{... | collective-permute-start | bytes 82952
  741.7 21.7 %copy-start.55 = (bf16[3,38809]{1,0:T(4,128)(2,1)S(1)}, bf16[3,38809]{1,0:T(4,128)(2,1)}, u32[]{:S(2)}) copy-start(bf16[3,38809]{1,0:T(4,128)(2,1)} %get-tuple-element.208) | copy-start | bytes 698566
  741.7 21.7 %copy-start.56 = (bf16[3,38809]{1,0:T(4,128)(2,1)S(1)}, bf16[3,38809]{1,0:T(4,128)(2,1)}, u32[]{:S(2)}) copy-start(bf16[3,38809]{1,0:T(4,128)(2,1)} %get-tuple-element.209) | copy-start | bytes 698566
  741.7 21.8 %copy-start.57 = (bf16[3,38809]{1,0:T(4,128)(2,1)S(1)}, bf16[3,38809]{1,0:T(4,128)(2,1)}, u32[]{:S(2)}) copy-start(bf16[3,38809]{1,0:T(4,128)(2,1)} %get-tuple-element.210) | copy-start | bytes 698566
  763.5 49.4 %copy-start.28 = (f32[200,768]{1,0:T(8,128)S(1)}, f32[200,768]{1,0:T(8,128)}, u32[]{:S(2)}) copy-start(f32[200,768]{1,0:T(8,128)} %copy-done.27) | copy-start | bytes 1843204
  785.5 30.3 %copy-start.7 = (bf16[197,768]{1,0:T(8,128)(2,1)S(1)}, bf16[197,768]{1,0:T(8,128)(2,1)}, u32[]{:S(2)}) copy-start(bf16[197,768]{1,0:T(8,128)(2,1)} %copy-done.6) | copy-start | bytes 907780
  785.5 30.3 %copy-start.9 = (bf16[197,768]{1,0:T(8,128)(2,1)S(1)}, bf16[197,768]{1,0:T(8,128)(2,1)}, u32[]{:S(2)}) copy-start(bf16[197,768]{1,0:T(8,128)(2,1)} %copy-done.8) | copy-start | bytes 907780
  785.5 30.3 %copy-start.60 = (f32[768]{0:T(1024)S(1)}, f32[768]{0:T(1024)}, u32[]{:S(2)}) copy-start(f32[768]{0:T(1024)} %param.24) | copy-start | bytes 9220
  785.5 30.3 %copy-start.66 = (f32[768]{0:T(1024)S(1)}, f32[768]{0:T(1024)}, u32[]{:S(2)}) copy-start(f32[768]{0:T(1024)} %param.25) | copy-start | bytes 9220
  785.5 30.2 %copy-start.70 = (pred[197]{0:T(512)(128)(4,1)S(1)}, pred[197]{0:T(512)(128)(4,1)}, u32[]{:S(2)}) copy-start(pred[197]{0:T(512)(128)(4,1)} %copy-done.69) | copy-start | bytes 595
  785.5 30.2 %copy-start.72 = (pred[197]{0:T(512)(128)(4,1)S(1)}, pred[197]{0:T(512)(128)(4,1)}, u32[]{:S(2)}) copy-start(pred[197]{0:T(512)(128)(4,1)} %copy-done.71) | copy-start | bytes 595
  785.5 30.2 %copy-start.74 = (f32[197]{0:T(256)S(1)}, f32[197]{0:T(256)}, u32[]{:S(2)}) copy-start(f32[197]{0:T(256)} %copy-done.73) | copy-start | bytes 2368
  785.6 30.2 %copy-start.76 = (f32[197]{0:T(256)S(1)}, f32[197]{0:T(256)}, u32[]{:S(2)}) copy-start(f32[197]{0:T(256)} %copy-done.75) | copy-start | bytes 2368
  785.6 30.2 %copy-start.79 = (f32[197]{0:T(256)S(1)}, f32[197]{0:T(256)}, u32[]{:S(2)}) copy-start(f32[197]{0:T(256)} %copy-done.78) | copy-start | bytes 2368
  785.6 30.2 %copy-start.81 = (f32[197]{0:T(256)S(1)}, f32[197]{0:T(256)}, u32[]{:S(2)}) copy-start(f32[197]{0:T(256)} %copy-done.80) | copy-start | bytes 2368
  785.6 32.3 %copy-start.11 = (f32[197,768]{1,0:T(8,128)S(1)}, f32[197,768]{1,0:T(8,128)}, u32[]{:S(2)}) copy-start(f32[197,768]{1,0:T(8,128)} %copy-done.10) | copy-start | bytes 1815556
  (77 other events, 294.6 us)
Sparse Core Ops, SparseCore 0:
  12.8 33.9 all-gather.20
  49.0 30.3 all-gather.16
  216.8 29.3 all-gather.22
  248.2 30.3 all-gather.18
  365.6 29.4 all-gather.28
  397.1 30.3 all-gather.24
  542.6 30.7 all-gather.26
  575.0 30.3 all-gather.30
  740.7 112.6 all-reduce.24
where the time goes:
time: 881 us; the launch traced here: 876 us
  blocking collectives  369 us (42%)
  waiting for transfers between devices  164 us (19%)
  matrix products  163 us (19%)
  local copies, waits for them, and re-layouts  116 us (13%)
  other arithmetic  26.8 us (3%)
  starting transfers between devices  22 us (2%)
  between operations  16.3 us (2%)
    unnamed x4, blocking collectives  305 us
    unnamed x251, local copies, waits for them, and re-layouts  64.5 us
    all_gather x2, waiting for transfers between devices, body(): second_full = lax.all_gather(second_low, 'narrow', axis=0, tiled=True)  54.3 us
    all_gather x2, waiting for transfers between devices, body(): mlp_grad_full = lax.all_gather(mlp_grad, 'narrow', axis=0, tiled=True)  49.8 us
    dot_general x2, matrix products, body(): jnp.einsum('kn,nb->kb', split_three(grid_grad), bucket_table, preferred_e...  43.7 us
    psum x1, blocking collectives, body(): lax.psum((small_total[0], small_total[1], small_total[2], small_total[3],...  39.8 us
    all_gather x2, waiting for transfers between devices, body(): attn_grad_full = lax.all_gather(attn_grad, 'narrow', axis=0, tiled=True)  31.7 us
    all_gather x2, waiting for transfers between devices, body(): first_full = lax.all_gather(first_low, 'narrow', axis=0, tiled=True)  25.9 us
  transfers between devices with their start and end apart: 17, of which 8 were waited for; matrix products, arithmetic and copies ran while one was open for 18% of the time, Pallas kernels for 0%

commit v1 on v0

v1 whole, which is shorter than its diff:
```python
import functools

import jax
import jax.numpy as jnp
from jax import lax
from jax.experimental import pallas as pl
from jax.experimental.pallas import tpu as pltpu
from jax.sharding import PartitionSpec as P


SEQ = 197
PAD = 208
LANES = 256
EPSILON = 1e-06
ROOT_HALF = 0.7071067811865476
DENSITY = 0.3989422804014327
CORE, SIDE, DEEP = 1, 2, 4
PIECES = 8
LOW = 32
NEGATIVE = -1e30
VMEM_LIMIT = 56 * 1024 * 1024
F32 = jnp.float32
BF16 = jnp.bfloat16

NN = (((1,), (0,)), ((), ()))
NT = (((1,), (1,)), ((), ()))
TN = (((0,), (0,)), ((), ()))


def mul(left, right, dims=NN):
    return lax.dot_general(left, right, dims, preferred_element_type=F32)


def vmem():
    return pl.BlockSpec(memory_space=pltpu.VMEM)


def anywhere():
    return pl.BlockSpec(memory_space=pl.ANY)


def scalars():
    return pl.BlockSpec(memory_space=pltpu.SMEM)


def call(kernel, name, outs, in_specs, out_specs=None, scratch=(), flops=0, nbytes=0):
    if out_specs is None:
        out_specs = [vmem()] * len(outs)
    return pl.pallas_call(
        kernel,
        out_shape=[jax.ShapeDtypeStruct(shape, dtype) for shape, dtype in outs],
        in_specs=in_specs,
        out_specs=out_specs,
        scratch_shapes=list(scratch),
        compiler_params=pltpu.CompilerParams(vmem_limit_bytes=VMEM_LIMIT),
        cost_estimate=pl.CostEstimate(flops=flops, bytes_accessed=nbytes, transcendentals=0),
        name=name,
    )


def norm_parts(values):
    center = values - jnp.mean(values, axis=-1, keepdims=True)
    spread = jnp.mean(center * center, axis=-1, keepdims=True)
    inverse = lax.rsqrt(spread + EPSILON)
    return center * inverse, inverse


def norm_back(grad, normed, inverse, gain):
    scaled = grad * gain
    inner = jnp.mean(scaled, axis=-1, keepdims=True)
    cross = jnp.mean(scaled * normed, axis=-1, keepdims=True)
    return inverse * (scaled - inner - normed * cross)


def col(values):
    return jnp.sum(values, axis=0, keepdims=True)


def first_kernel(tok_ref, mask_ref, vec_ref, out_ref):
    width = tok_ref.shape[1]
    masked = jnp.where(mask_ref[...] > 0.0, vec_ref[0:1, :], tok_ref[...].astype(F32))
    normed, _ = norm_parts(masked)
    out = normed * vec_ref[1:2, :] + vec_ref[2:3, :]
    rows = lax.broadcasted_iota(jnp.int32, (tok_ref.shape[0], 1), 0)
    real = lax.rem(rows, PAD) < SEQ
    out_ref[...] = jnp.where(real, out, 0.0).astype(BF16)


def bias_kernel(buckets_ref, table_ref, out_ref):
    heads, parts, _ = table_ref.shape
    for half in range(2):
        lanes = pl.ds(half * 128, 128)
        index = buckets_ref[:, lanes]
        low = lax.bitwise_and(index, 127)
        high = lax.shift_right_logical(index, 7)
        column = lax.broadcasted_iota(jnp.int32, index.shape, 1) + half * 128
        for head in range(heads):
            total = jnp.full(index.shape, NEGATIVE, F32)
            for part in range(parts):
                row = jnp.broadcast_to(table_ref[head, part : part + 1, :], index.shape)
                found = jnp.take_along_axis(row, low, axis=1, mode="promise_in_bounds")
                total = jnp.where(high == part, found, total)
            out_ref[head, :, lanes] = jnp.where(column < SEQ, total, NEGATIVE)


def copies_in(w_ref, pieces, slot, target, sem):
    rows = target.shape[0] // PIECES
    half = rows // 2
    place = w_ref[0]
    made = []
    for piece, (first, count, ref) in zip(
        (0, 1, 2, 3, 4, 5, 6, 6, 7, 7),
        [(0, rows, r) for r in pieces[:6]]
        + [(0, half, pieces[6]), (half, half, pieces[7]), (0, half, pieces[8]), (half, half, pieces[9])],
        strict=True,
    ):
        start = pl.multiple_of(lax.bitwise_xor(place, piece) * rows, rows) + first
        made.append(
            pltpu.make_async_copy(
                ref.at[slot], target.at[pl.ds(pl.multiple_of(start, 16), count), :], sem
            )
        )
    return made


def load_weights(w_ref, refs, slot, target, sem):
    if len(refs) == 1:
        return [pltpu.make_async_copy(refs[0], target, sem)]
    return copies_in(w_ref, refs, slot, target, sem)


def go(copies):
    for c in copies:
        c.start()


def finish(copies):
    for c in copies:
        c.wait()


def attend_kernel(n_weights, slot, first, *refs):
    w_ref = refs[0]
    weights = refs[1 : 1 + n_weights]
    rest = refs[1 + n_weights :]
    x_ref, shift_ref, bias_ref = rest[:3]
    rest = rest[3:]
    if not first:
        acc_in = rest[0]
        rest = rest[1:]
    acc_ref, qkv_ref, probs_ref, mixed_ref, mat, sem = rest
    copies = load_weights(w_ref, weights, slot, mat, sem)
    go(copies)
    finish(copies)
    width = mat.shape[0]
    local = width // 4
    heads = bias_ref.shape[0]
    size = local // heads
    qkv = mul(x_ref[...], mat[: 3 * local, :], NT) + shift_ref[...]
    queries = (qkv[:, :local].astype(BF16).astype(F32) * size ** (-0.5)).astype(BF16)
    keys = qkv[:, local : 2 * local].astype(BF16)
    values = qkv[:, 2 * local :].astype(BF16)
    qkv_ref[0] = queries
    qkv_ref[1] = keys
    qkv_ref[2] = values
    lane = lax.broadcasted_iota(jnp.int32, (PAD, local), 1)
    pages = x_ref.shape[0] // PAD
    zero = jnp.zeros((PAD, local), BF16)
    for page in range(pages):
        rows = slice(page * PAD, (page + 1) * PAD)
        q, k, v = queries[rows], keys[rows], values[rows]
        mixed = jnp.zeros((PAD, local), F32)
        for head in range(heads):
            own = (lane >= head * size) & (lane < (head + 1) * size)
            scores = mul(jnp.where(own, q, zero), k, NT) + bias_ref[head][:, :PAD]
            top = jnp.max(scores, axis=1, keepdims=True)
            power = jnp.exp(scores - top)
            total = jnp.sum(power, axis=1, keepdims=True)
            probs = (power * (1.0 / total)).astype(BF16)
            probs_ref[page * heads + head] = probs
            mixed = mixed + mul(probs, jnp.where(own, v, zero))
        mixed_ref[rows, :] = mixed.astype(BF16)
    out = mul(mixed_ref[...], mat[3 * local :, :])
    acc_ref[...] = out if first else acc_in[...] + out


def middle_kernel(acc_ref, tok_ref, mask_ref, grad_ref, vec_ref, mid_ref, x_ref, mg_ref):
    masked = jnp.where(mask_ref[...] > 0.0, vec_ref[0:1, :], tok_ref[...].astype(F32))
    middle = masked + vec_ref[2:3, :] * (acc_ref[...] + vec_ref[1:2, :])
    mid_ref[...] = middle
    normed, _ = norm_parts(middle)
    x_ref[...] = (normed * vec_ref[3:4, :] + vec_ref[4:5, :]).astype(BF16)
    mg_ref[...] = (grad_ref[...].astype(F32) * vec_ref[5:6, :]).astype(BF16)


def copies_out(w_ref, mats, keep, send, sem):
    place = w_ref[0]
    made = []
    for number, mat in enumerate(mats):
        rows = mat.shape[0] // PIECES
        for piece in range(PIECES):
            start = pl.multiple_of(lax.bitwise_xor(place, piece) * rows, rows)
            target = send if piece & CORE else keep
            made.append(
                pltpu.make_async_copy(
                    mat.at[pl.ds(start, rows), :], target.at[piece >> 1, number], sem
                )
            )
    return made


def mlp_kernel(n_weights, slot, first, *refs):
    w_ref = refs[0]
    in_refs = refs[1 : 1 + n_weights]
    down_refs = refs[1 + n_weights : 1 + 2 * n_weights]
    rest = refs[1 + 2 * n_weights :]
    x_ref, mg_ref, shift_ref = rest[:3]
    rest = rest[3:]
    if not first:
        out_in, grad_in = rest[:2]
        rest = rest[2:]
    out_ref, grad_ref, col_ref, keep, send, in_mat, down_mat, in_grad, down_grad, sem, osem = rest
    copies = load_weights(w_ref, in_refs, slot, in_mat, sem.at[0]) + load_weights(
        w_ref, down_refs, slot, down_mat, sem.at[1]
    )
    go(copies)
    finish(copies)
    width = in_mat.shape[0]
    x = x_ref[...]
    mg = mg_ref[...]
    out = None
    back = None
    for start in range(0, width, 256):
        units = slice(start, start + 256)
        weight_in = in_mat[:, units]
        weight_down = down_mat[units, :]
        pre = mul(x, weight_in) + shift_ref[:, units]
        phi = 0.5 * (1.0 + lax.erf(pre * ROOT_HALF))
        hidden = (pre * phi).astype(BF16)
        slope = phi + pre * (DENSITY * jnp.exp(-0.5 * pre * pre))
        part = mul(hidden, weight_down)
        out = part if out is None else out + part
        hidden_grad = mul(mg, weight_down, NT)
        pre_grad = hidden_grad * slope
        low = pre_grad.astype(BF16)
        col_ref[:, units] = col(low.astype(F32))
        part = mul(low, weight_in, NT)
        back = part if back is None else back + part
        down_grad[units, :] = mul(hidden, mg, TN).astype(BF16)
        in_grad[:, units] = mul(x, low, TN).astype(BF16)
    out_ref[...] = out if first else out_in[...] + out
    grad_ref[...] = back if first else grad_in[...] + back
    copies = copies_out(w_ref, [in_grad, down_grad], keep, send, osem)
    go(copies)
    finish(copies)


def turn_kernel(mid_ref, out_ref, back_ref, grad_ref, acc_ref, vec_ref, layer_ref, mgrad_ref, ag_ref, sums_ref):
    middle = mid_ref[...]
    grad = grad_ref[...].astype(F32)
    mlp_out = out_ref[...] + vec_ref[1:2, :]
    layer_ref[...] = (middle + vec_ref[2:3, :] * mlp_out).astype(BF16)
    normed, inverse = norm_parts(middle)
    second = back_ref[...]
    middle_grad = grad + norm_back(second, normed, inverse, vec_ref[0:1, :])
    mgrad_ref[...] = middle_grad
    scaled = middle_grad * vec_ref[3:4, :]
    ag_ref[...] = scaled.astype(BF16)
    sums_ref[0:1, :] = col(scaled)
    sums_ref[1:2, :] = col(middle_grad * (acc_ref[...] + vec_ref[4:5, :]))
    sums_ref[2:3, :] = col(second * normed)
    sums_ref[3:4, :] = col(second)
    sums_ref[4:5, :] = col(grad * vec_ref[2:3, :])
    sums_ref[5:6, :] = col(grad * mlp_out)
    sums_ref[6:8, :] = jnp.zeros_like(sums_ref[6:8, :])


def attend_back_kernel(n_weights, slot, first, *refs):
    w_ref = refs[0]
    weights = refs[1 : 1 + n_weights]
    rest = refs[1 + n_weights :]
    x_ref, ag_ref, qkv_ref, probs_ref, mixed_ref = rest[:5]
    rest = rest[5:]
    if not first:
        grad_in = rest[0]
        rest = rest[1:]
    grad_ref, col_ref, grid_ref, keep, send, mat, mat_grad, dqkv, sem, osem = rest
    copies = load_weights(w_ref, weights, slot, mat, sem)
    go(copies)
    finish(copies)
    width = mat.shape[0]
    local = width // 4
    heads = grid_ref.shape[0]
    size = local // heads
    ag = ag_ref[...]
    mixed_grad = mul(ag, mat[3 * local :, :], NT).astype(BF16)
    mat_grad[3 * local :, :] = mul(mixed_ref[...], ag, TN).astype(BF16)
    lane = lax.broadcasted_iota(jnp.int32, (PAD, local), 1)
    pages = x_ref.shape[0] // PAD
    zero = jnp.zeros((PAD, local), BF16)
    for page in range(pages):
        rows = slice(page * PAD, (page + 1) * PAD)
        q, v, dm = qkv_ref[0, rows, :], qkv_ref[2, rows, :], mixed_grad[rows]
        k = (qkv_ref[1, rows, :].astype(F32) * size ** (-0.5)).astype(BF16)
        dq = jnp.zeros((PAD, local), F32)
        dk = jnp.zeros((PAD, local), F32)
        dv = jnp.zeros((PAD, local), F32)
        for head in range(heads):
            own = (lane >= head * size) & (lane < (head + 1) * size)
            dmh = jnp.where(own, dm, zero)
            probs_low = probs_ref[page * heads + head]
            probs = probs_low.astype(F32)
            weighed = probs * mul(dmh, v, NT)
            score = weighed - probs * jnp.sum(weighed, axis=1, keepdims=True)
            low = score.astype(BF16)
            if page == 0:
                grid_ref[head] = low.astype(F32)
            else:
                grid_ref[head] = grid_ref[head] + low.astype(F32)
            dq = dq + mul(low, jnp.where(own, k, zero))
            dk = dk + mul(low, jnp.where(own, q, zero), TN)
            dv = dv + mul(probs_low, dmh, TN)
        dqkv[rows, :] = jnp.concatenate([dq, dk, dv], axis=1).astype(BF16)
    grads = dqkv[...]
    col_ref[...] = col(grads.astype(F32))
    mat_grad[: 3 * local, :] = mul(grads, x_ref[...], TN).astype(BF16)
    back = mul(grads, mat[: 3 * local, :])
    grad_ref[...] = back if first else grad_in[...] + back
    copies = copies_out(w_ref, [mat_grad], keep, send, osem)
    go(copies)
    finish(copies)


def last_kernel(tok_ref, mask_ref, mgrad_ref, first_ref, vec_ref, grad_ref, sums_ref):
    mask = mask_ref[...] > 0.0
    masked = jnp.where(mask, vec_ref[0:1, :], tok_ref[...].astype(F32))
    normed, inverse = norm_parts(masked)
    first = first_ref[...]
    in_grad = mgrad_ref[...] + norm_back(first, normed, inverse, vec_ref[1:2, :])
    grad_ref[...] = jnp.where(mask, 0.0, in_grad).astype(BF16)
    sums_ref[0:1, :] = col(jnp.where(mask, in_grad, 0.0))
    sums_ref[1:2, :] = col(first * normed)
    sums_ref[2:3, :] = col(first)
    sums_ref[3:8, :] = jnp.zeros_like(sums_ref[3:8, :])


def table_kernel(grid_count, *refs):
    buckets_ref = refs[0]
    grids = refs[1 : 1 + grid_count]
    out_ref = refs[1 + grid_count]
    heads = grids[0].shape[0]
    highs = out_ref.shape[0] // (grid_count * heads)
    out_ref[...] = jnp.zeros_like(out_ref)

    def step(block, _):
        base = pl.multiple_of(block * 8, 8)
        index = buckets_ref[pl.ds(base, 8), :][:, :PAD]
        loads = [[g[h, pl.ds(base, 8), :] for h in range(heads)] for g in grids]
        total = None
        for row in range(8):
            one = index[row : row + 1]
            low = lax.bitwise_and(one, LOW - 1)
            high = lax.shift_right_logical(one, 5)
            right = (
                jnp.broadcast_to(low, (LOW, PAD)) == lax.broadcasted_iota(jnp.int32, (LOW, PAD), 0)
            ).astype(F32).astype(BF16)
            match = jnp.broadcast_to(high, (highs, PAD)) == lax.broadcasted_iota(
                jnp.int32, (highs, PAD), 0
            )
            left = jnp.concatenate(
                [
                    jnp.where(match, jnp.broadcast_to(loads[g][h][row : row + 1], (highs, PAD)), 0.0)
                    for g in range(grid_count)
                    for h in range(heads)
                ],
                axis=0,
            ).astype(BF16)
            part = mul(left, right, NT)
            total = part if total is None else total + part
        out_ref[...] += total
        return 0

    lax.fori_loop(0, PAD // 8, step, 0)


def assemble(w_ref, pieces, number, place_in):
    for piece, ref in enumerate(pieces):
        rows = place_in.shape[0] // PIECES
        start = pl.multiple_of(lax.bitwise_xor(w_ref[0], piece) * rows, rows)
        place_in[pl.ds(start, rows), :] = ref[number].astype(F32)


def mlp_final_kernel(w_ref, *refs):
    pieces, (in_ref, down_ref) = refs[:PIECES], refs[PIECES:]
    assemble(w_ref, pieces, 0, in_ref)
    assemble(w_ref, pieces, 1, down_ref)


def attend_final_kernel(w_ref, *refs):
    pieces, (qkv_ref, out_ref, whole) = refs[:PIECES], refs[PIECES:]
    assemble(w_ref, pieces, 0, whole)
    cut = qkv_ref.shape[0]
    qkv_ref[...] = whole[:cut, :]
    out_ref[...] = whole[cut:, :]


def across(values, bit):
    count = lax.axis_size("wide")
    return lax.ppermute(values, "wide", [(i, i ^ bit) for i in range(count)])


def along(values, step):
    count = lax.axis_size("narrow")
    return lax.ppermute(values, "narrow", [(i, (i + step) % count) for i in range(count)])


def gather_shards(piece, count):
    half = piece.shape[0] // 2
    zero = jnp.stack([along(piece, -step) for step in range(1, count)])
    side, deep = across(zero, SIDE), across(zero, DEEP)
    far_a = across(side[:, :half], DEEP)
    far_b = across(deep[:, half:], SIDE)
    found = [zero, side, deep, far_a, far_b]
    other = [across(a, CORE) for a in found]
    return [found[0], other[0], found[1], other[1], found[2], other[2], found[3], found[4], other[3], other[4]]


def add_low(left, right):
    return (left.astype(F32) + right.astype(F32)).astype(BF16)


def reduce_plane(keep, send, side_first):
    other = across(send, CORE)
    if side_first:
        stay = add_low(jnp.stack([keep[0], keep[2]]), jnp.stack([other[0], other[2]]))
        leave = add_low(jnp.stack([keep[1], keep[3]]), jnp.stack([other[1], other[3]]))
        bits = (SIDE, DEEP)
    else:
        stay = add_low(keep[:2], other[:2])
        leave = add_low(keep[2:], other[2:])
        bits = (DEEP, SIDE)
    other = across(leave, bits[0])
    stay_one = add_low(stay[0], other[0])
    leave_one = add_low(stay[1], other[1])
    return add_low(stay_one, across(leave_one, bits[1]))


def rest_of_wide(values):
    bit = PIECES
    while bit < lax.axis_size("wide"):
        values = (values.astype(F32) + across(values, bit).astype(F32)).astype(values.dtype)
        bit *= 2
    return values


def gather_wide(values):
    half = values.shape[1] // 2
    side, deep = across(values, SIDE), across(values, DEEP)
    far = jnp.concatenate(
        [across(side[:, :half], DEEP), across(deep[:, half:], SIDE)], axis=1
    )
    found = [values, side, deep, far]
    other = [across(a, CORE) for a in found]
    return [a for pair in zip(found, other, strict=True) for a in pair]


def body(
    tokens,
    page_mask,
    buckets,
    mask_token,
    first_gain,
    first_shift,
    qkv_weight,
    query_bias,
    value_bias,
    position_bias,
    out_weight,
    out_bias,
    attn_scale,
    second_gain,
    second_shift,
    in_weight,
    in_bias,
    down_weight,
    down_bias,
    mlp_scale,
    out_grad,
):
    pages, seq, width = tokens.shape
    count = lax.axis_size("narrow")
    local = qkv_weight.shape[2]
    heads, bucket_count = position_bias.shape
    rows = pages * PAD
    piece_rows = width // PIECES
    place = lax.bitwise_and(lax.axis_index("wide").astype(jnp.int32), PIECES - 1)
    place_ref = place.reshape(1)

    attn_own = jnp.concatenate(
        [qkv_weight.transpose(1, 2, 0).reshape(3 * local, width), out_weight], axis=0
    )
    own = [attn_own, in_weight, down_weight]
    gathered = [
        gather_shards(lax.dynamic_slice(mat, (place * piece_rows, 0), (piece_rows, width)), count)
        for mat in own
    ]

    tables = jnp.pad(position_bias, ((0, 0), (0, width - bucket_count)))
    small = jnp.concatenate(
        [query_bias, value_bias, in_bias, tables.reshape(-1)]
    ).reshape(-1, 128)
    smalls = [small] + [along(small, -step) for step in range(1, count)]
    qkv_shifts, in_shifts, table_parts = [], [], []
    for one in smalls:
        flat = one.reshape(-1)
        qkv_shifts.append(
            jnp.concatenate([flat[:local], jnp.zeros((local,), F32), flat[local : 2 * local]])[None]
        )
        in_shifts.append(flat[2 * local : 2 * local + width][None])
        table_parts.append(flat[2 * local + width :].reshape(heads, width // 128, 128))

    fill = ((0, 0), (0, PAD - seq), (0, 0))
    tok = jnp.pad(tokens, fill).reshape(rows, width)
    grad = jnp.pad(out_grad, fill).reshape(rows, width)
    flags = (page_mask > 0) & (jnp.arange(seq, dtype=jnp.int32) % SEQ != 0)
    mask = jnp.pad(flags.astype(F32), ((0, 0), (0, PAD - seq))).reshape(rows, 1)
    index = jnp.pad(buckets, ((0, PAD - seq), (0, LANES - seq)))
    wide_shape = (rows, width)

    x_one = call(first_kernel, "first", [(wide_shape, BF16)], [vmem()] * 3)(
        tok, mask, jnp.stack([mask_token, first_gain, first_shift])
    )[0]
    biases = [
        call(bias_kernel, f"bias{d}", [((heads, PAD, LANES), F32)], [vmem()] * 2)(index, t)[0]
        for d, t in enumerate(table_parts)
    ]

    acc = None
    kept = []
    for d in range(count):
        weights = [attn_own] if d == 0 else gathered[0]
        first = acc is None
        more = [] if first else [acc]
        acc, qkv, probs, mixed = call(
            functools.partial(attend_kernel, len(weights), d - 1, first),
            f"attend{d}",
            [
                (wide_shape, F32),
                ((3, rows, local), BF16),
                ((pages * heads, PAD, PAD), BF16),
                ((rows, local), BF16),
            ],
            [scalars()] + [anywhere()] * len(weights) + [vmem()] * (3 + len(more)),
            scratch=[pltpu.VMEM((width, width), BF16), pltpu.SemaphoreType.DMA],
            flops=2 * rows * width * width + pages * heads * PAD * PAD * 1024,
            nbytes=2 * width * width,
        )(place_ref, *weights, x_one, qkv_shifts[d], biases[d], *more)
        kept.append((qkv, probs, mixed))

    middle, x_two, mlp_grad = call(
        middle_kernel, "middle", [(wide_shape, F32), (wide_shape, BF16), (wide_shape, BF16)], [vmem()] * 5
    )(
        acc,
        tok,
        mask,
        grad,
        jnp.stack([mask_token, out_bias, attn_scale, second_gain, second_shift, mlp_scale]),
    )

    out_sum = back_sum = None
    in_cols, mlp_pieces = [], []
    for d in range(count):
        in_ws = [in_weight] if d == 0 else gathered[1]
        down_ws = [down_weight] if d == 0 else gathered[2]
        first = out_sum is None
        more = [] if first else [out_sum, back_sum]
        out_sum, back_sum, in_col, keep, send = call(
            functools.partial(mlp_kernel, len(in_ws), d - 1, first),
            f"mlp{d}",
            [
                (wide_shape, F32),
                (wide_shape, F32),
                ((1, width), F32),
                ((4, 2, piece_rows, width), BF16),
                ((4, 2, piece_rows, width), BF16),
            ],
            [scalars()] + [anywhere()] * (2 * len(in_ws)) + [vmem()] * (3 + len(more)),
            out_specs=[vmem()] * 3 + [anywhere()] * 2,
            scratch=[pltpu.VMEM((width, width), BF16)] * 4
            + [pltpu.SemaphoreType.DMA((2,)), pltpu.SemaphoreType.DMA],
            flops=12 * rows * width * width,
            nbytes=2 * width * width,
        )(place_ref, *in_ws, *down_ws, x_two, mlp_grad, in_shifts[d], *more)
        in_cols.append(in_col)
        mlp_pieces.append(reduce_plane(keep, send, d % 2 == 0))

    layer, middle_grad, attn_grad, mid_sums = call(
        turn_kernel,
        "turn",
        [(wide_shape, BF16), (wide_shape, F32), (wide_shape, BF16), ((8, width), F32)],
        [vmem()] * 6,
    )(
        middle,
        out_sum,
        back_sum,
        grad,
        acc,
        jnp.stack([second_gain, down_bias, mlp_scale, attn_scale, out_bias]),
    )

    first_sum = None
    qkv_cols, grids = [None] * count, [None] * count
    attn_pieces = [None] * count
    for d in list(range(1, count)) + [0]:
        weights = [attn_own] if d == 0 else gathered[0]
        first = first_sum is None
        more = [] if first else [first_sum]
        first_sum, qkv_cols[d], grids[d], keep, send = call(
            functools.partial(attend_back_kernel, len(weights), d - 1, first),
            f"attend_back{d}",
            [
                (wide_shape, F32),
                ((1, 3 * local), F32),
                ((heads, PAD, PAD), F32),
                ((4, 1, piece_rows, width), BF16),
                ((4, 1, piece_rows, width), BF16),
            ],
            [scalars()] + [anywhere()] * len(weights) + [vmem()] * (5 + len(more)),
            out_specs=[vmem()] * 3 + [anywhere()] * 2,
            scratch=[
                pltpu.VMEM((width, width), BF16),
                pltpu.VMEM((width, width), BF16),
                pltpu.VMEM((rows, 3 * local), BF16),
                pltpu.SemaphoreType.DMA,
                pltpu.SemaphoreType.DMA,
            ],
            flops=4 * rows * width * width + pages * heads * PAD * PAD * 2048,
            nbytes=2 * width * width,
        )(place_ref, *weights, x_one, attn_grad, *kept[d], *more)
        attn_pieces[d] = reduce_plane(keep, send, d % 2 == 0)

    tok_grad, last_sums = call(
        last_kernel, "last", [(wide_shape, BF16), ((8, width), F32)], [vmem()] * 5
    )(tok, mask, middle_grad, first_sum, jnp.stack([mask_token, first_gain]))

    highs = width // LOW
    table = call(
        functools.partial(table_kernel, count),
        "table",
        [((count * heads * highs, LOW), F32)],
        [vmem()] * (1 + count),
        flops=2 * count * heads * highs * PAD * PAD * 128,
    )(index, *grids)[0]

    shared = jnp.concatenate([last_sums[:3], mid_sums[:6]], axis=0).reshape(-1)
    table_rows = table.reshape(count, heads * width)
    own_parts = [
        jnp.concatenate(
            [
                qkv_cols[d][0, :local],
                qkv_cols[d][0, 2 * local :],
                in_cols[d][0],
                table_rows[d],
            ]
        )
        for d in range(count)
    ]
    flat = jnp.concatenate([shared] + own_parts).reshape(-1, 128)
    for bit in (CORE, SIDE, DEEP):
        flat = flat + across(flat, bit)
    flat = rest_of_wide(flat).reshape(-1)
    size, part = shared.shape[0], own_parts[0].shape[0]
    total = flat[: size + part]
    for step in range(1, count):
        sent = jnp.concatenate([flat[:size], flat[size + step * part : size + (step + 1) * part]])
        total = total + along(sent.reshape(-1, 128), step).reshape(-1)
    sums = total[:size].reshape(9, width)
    part_sums = total[size:]

    def finish_pieces(pieces):
        done = pieces[0].astype(F32)
        for step in range(1, count):
            done = done + along(pieces[step], step).astype(F32)
        return gather_wide(rest_of_wide(done.astype(BF16)))

    in_w_grad, down_w_grad = call(
        mlp_final_kernel,
        "mlp_final",
        [((width, width), F32)] * 2,
        [scalars()] + [vmem()] * PIECES,
    )(place_ref, *finish_pieces(mlp_pieces))
    qkv_w_grad, out_w_grad = call(
        attend_final_kernel,
        "attend_final",
        [((3 * local, width), F32), ((local, width), F32)],
        [scalars()] + [vmem()] * PIECES,
        scratch=[pltpu.VMEM((width, width), F32)],
    )(place_ref, *finish_pieces(attn_pieces))

    return (
        layer.reshape(pages, PAD, width)[:, :seq],
        tok_grad.reshape(pages, PAD, width)[:, :seq],
        sums[0],
        sums[1],
        sums[2],
        qkv_w_grad.reshape(3, local, width).transpose(2, 0, 1),
        part_sums[:local],
        part_sums[local : 2 * local],
        part_sums[2 * local + width :].reshape(heads, width)[:, :bucket_count],
        out_w_grad,
        sums[3],
        sums[4],
        sums[5],
        sums[6],
        in_w_grad,
        part_sums[2 * local : 2 * local + width],
        down_w_grad,
        sums[7],
        sums[8],
    )


def solution(mesh):
    placed = (
        P(None, ("wide", "narrow"), None),
        P(None, ("wide", "narrow")),
        P(),
        P(),
        P(),
        P(),
        P(None, None, "narrow"),
        P("narrow"),
        P("narrow"),
        P("narrow", None),
        P("narrow", None),
        P(),
        P(),
        P(),
        P(),
        P(None, "narrow"),
        P("narrow"),
        P("narrow", None),
        P(),
        P(),
        P(None, ("wide", "narrow"), None),
    )
    return jax.shard_map(
        body,
        mesh=mesh,
        in_specs=placed,
        out_specs=(
            P(None, ("wide", "narrow"), None),
            P(None, ("wide", "narrow"), None),
            P(),
            P(),
            P(),
            P(None, None, "narrow"),
            P("narrow"),
            P("narrow"),
            P("narrow", None),
            P("narrow", None),
            P(),
            P(),
            P(),
            P(),
            P(None, "narrow"),
            P("narrow"),
            P("narrow", None),
            P(),
            P(),
        ),
        check_vma=False,
    )
```

time: 881 us -> 421 us (0.48)
  blocking collectives: 369 us -> 0 us
  matrix products: 163 us -> 0 us
  Pallas kernels: 0 us -> 159 us
  starting transfers between devices: 22 us -> 102 us
  local copies, waits for them, and re-layouts: 116 us -> 41.7 us
  waiting for transfers between devices: 164 us -> 97.2 us
  other arithmetic: 26.8 us -> 12.7 us
  between operations: 16.3 us -> 2.43 us
    unnamed x4 -> x0, blocking collectives: 305 us -> none
    dot_general x41 -> x0, matrix products: 163 us -> none  [the longest x2 43.7 us: body(): jnp.einsum('kn,nb->kb', split_three(grid_grad), bucket_table, preferred_e...]
    all_gather x8 -> x0, waiting for transfers between devices: 162 us -> none  [the longest x2 54.3 us: body(): second_full = lax.all_gather(second_low, 'narrow', axis=0, tiled=True)]
    pallas_call x0 -> x23, Pallas kernels: none -> 159 us  [the longest x4 42.3 us: body(): call(functools.partial(mlp_kernel, len(in_ws), d - 1, first), f'mlp{d}',...]
    ppermute x0 -> x91, starting transfers between devices: none -> 102 us  [the longest x70 51.6 us: across(): return lax.ppermute(values, 'wide', [(i, i ^ bit) for i in range(count)])]
    ppermute x0 -> x91, waiting for transfers between devices: none -> 97.2 us  [the longest x70 83.2 us: across(): return lax.ppermute(values, 'wide', [(i, i ^ bit) for i in range(count)])]
    psum x2 -> x0, blocking collectives: 63.4 us -> none  [the longest x1 39.8 us: body(): lax.psum((small_total[0], small_total[1], small_total[2], small_total[3],...]
    unnamed x251 -> x176, local copies, waits for them, and re-layouts: 64.5 us -> 8.22 us
  transfers between devices with their start and end apart: 17 -> 91, of which waited for: 8 -> 28; matrix products, arithmetic and copies ran while one was open for 18% -> 12% of each run, Pallas kernels for 0% -> 37%
where the time goes in v1:
time: 421 us; the launch traced here: 415 us
  Pallas kernels  159 us (38%)
  starting transfers between devices  102 us (24%)
  waiting for transfers between devices  97.2 us (23%)
  local copies, waits for them, and re-layouts  41.7 us (10%)
  other arithmetic  12.7 us (3%)
    ppermute x70, waiting for transfers between devices, across(): return lax.ppermute(values, 'wide', [(i, i ^ bit) for i in range(count)])  83.2 us
    ppermute x70, starting transfers between devices, across(): return lax.ppermute(values, 'wide', [(i, i ^ bit) for i in range(count)])  51.6 us
    ppermute x21, starting transfers between devices, along(): lax.ppermute(values, 'narrow', [(i, (i + step) % count) for i in range(co...  50.3 us
    pallas_call x4, Pallas kernels, body(): call(functools.partial(mlp_kernel, len(in_ws), d - 1, first), f'mlp{d}',...  42.3 us
    pallas_call x4, Pallas kernels, body(): call(functools.partial(attend_back_kernel, len(weights), d - 1, first), f...  35.2 us
    pallas_call x4, Pallas kernels, body(): call(functools.partial(attend_kernel, len(weights), d - 1, first), f'atte...  26.5 us
    pallas_call x4, Pallas kernels, body(): call(bias_kernel, f'bias{d}', [((heads, PAD, LANES), F32)], [vmem()] * 2)  17.8 us
    pallas_call x1, Pallas kernels, body(): call(functools.partial(table_kernel, count), 'table', [((count * heads *...  14.2 us
  transfers between devices with their start and end apart: 91, of which 28 were waited for; matrix products, arithmetic and copies ran while one was open for 12% of the time, Pallas kernels for 37%

profile of v1, /device:TPU:0, one launch (start us, length us, event | category | flops | bytes accessed | tf_op | source)
XLA Modules:
  0.0 414.9 jit_solution(13326030888936341555)
XLA Ops:
  1.8 5.1 %collective-permute-start = (bf16[96,768]{1,0:T(8,128)(2,1)S(1)}, bf16[96,768]{1,0:T(8,128)(2,1)S(1)}, u32[]{:S(2)}, u32[]{:S(2)}) collective-permute-start(bf16[96,768]{1,0:T(8,128)(2,1)S(1)} %fusion.16), channel_id=1, source_target_pairs={{0,3},{1,0},{2,1},{3,2},{4,7},{5,4},{6,5},{7,6},{8,11},{9,8},{10,9... | collective-permute-start | bytes 442376 | tf_op jit(solution)/shard_map/ppermute | solution.py:414
  9.5 2.8 collective-permute-start.15
  23.9 4.5 %bias0.1.refs_4_ = f32[3,208,256]{2,1,0:T(8,128)} custom-call(s32[208,256]{1,0:T(8,128)} %pad.23.buckets_ref.refs_0_, f32[3,6,128]{2,1,0:T(8,128)} %reshape_reshape.3.table_ref), custom_call_target="tpu_custom_call" | custom-call | tf_op jit(solution)/shard_map/bias0/pallas_call | solution.py:534
  28.4 2.7 first.1.refs_2_.refs_11_
  31.1 3.8 collective-permute-start.14
  41.9 2.4 collective-permute-start.29
  44.4 6.3 %collective-permute-done.28 = bf16[96,768]{1,0:T(8,128)(2,1)S(1)} collective-permute-done((bf16[96,768]{1,0:T(8,128)(2,1)S(1)}, bf16[96,768]{1,0:T(8,128)(2,1)S(1)}, u32[]{:S(2)}, u32[]{:S(2)}) %collective-permute-start.28) | collective-permute-done | bytes 147488 | tf_op jit(solution)/shard_map/ppermute | solution.py:414
  51.2 2.5 collective-permute-start.21
  60.5 2.9 collective-permute-done.21.refs_5_
  64.3 2.4 collective-permute-start.9
  66.7 3.3 collective-permute-done.31.refs_13_
  72.9 2.4 collective-permute-start.24
  78.2 3.2 collective-permute-done.23.refs_7_
  86.0 6.2 %attend0.1 = (f32[416,768]{1,0:T(8,128)}, bf16[3,416,192]{2,1,0:T(8,128)(2,1)}, bf16[6,208,208]{2,1,0:T(8,128)(2,1)}, bf16[416,192]{1,0:T(8,128)(2,1)}) custom-call(s32[1]{0:T(128)} %bitcast.refs_0_.w_ref, bf16[768,768]{1,0:T(8,128)(2,1)} %pad_maximum_fusion.refs_1_, bf16[416,768]{1,0:T(8,128)(2,1)} %first.1.refs_2_.refs_11_, ...), custom_call_target="tpu_custom_call" | custom-call | flops 756547584 | bytes 1179648 | tf_op jit(solution)/shard_map/attend0/pallas_call | solution.py:544
  93.5 4.5 %bias1.1.refs_13_ = f32[3,208,256]{2,1,0:T(8,128)} custom-call(s32[208,256]{1,0:T(8,128)} %pad.23.buckets_ref.refs_0_, f32[3,6,128]{2,1,0:T(8,128)} %reshape.794.table_ref), custom_call_target="tpu_custom_call" | custom-call | tf_op jit(solution)/shard_map/bias1/pallas_call | solution.py:534
  99.2 4.5 %bias2.1.refs_13_ = f32[3,208,256]{2,1,0:T(8,128)} custom-call(s32[208,256]{1,0:T(8,128)} %pad.23.buckets_ref.refs_0_, f32[3,6,128]{2,1,0:T(8,128)} %reshape.792.table_ref), custom_call_target="tpu_custom_call" | custom-call | tf_op jit(solution)/shard_map/bias2/pallas_call | solution.py:534
  104.8 4.5 %bias3.1.refs_13_ = f32[3,208,256]{2,1,0:T(8,128)} custom-call(s32[208,256]{1,0:T(8,128)} %pad.23.buckets_ref.refs_0_, f32[3,6,128]{2,1,0:T(8,128)} %reshape.790.table_ref), custom_call_target="tpu_custom_call" | custom-call | tf_op jit(solution)/shard_map/bias3/pallas_call | solution.py:534
  111.0 6.7 %attend1.1 = (f32[416,768]{1,0:T(8,128)}, bf16[3,416,192]{2,1,0:T(8,128)(2,1)}, bf16[6,208,208]{2,1,0:T(8,128)(2,1)}, bf16[416,192]{1,0:T(8,128)(2,1)}) custom-call(s32[1]{0:T(128)} %bitcast.refs_0_.w_ref, bf16[3,96,768]{2,1,0:T(8,128)(2,1)} %copy-done, bf16[3,96,768]{2,1,0:T(8,128)(2,1)} %copy-done.3, bf16[3,96,768]{2,1,0:T(8,128)(2,1)} %copy-done.1, ...), custom_call_target="tpu_custom_call" | custom-call | flops 756547584 | bytes 1179648 | tf_op jit(solution)/shard_map/attend1/pallas_call | solution.py:544
  117.7 6.7 %attend2.1 = (f32[416,768]{1,0:T(8,128)}, bf16[3,416,192]{2,1,0:T(8,128)(2,1)}, bf16[6,208,208]{2,1,0:T(8,128)(2,1)}, bf16[416,192]{1,0:T(8,128)(2,1)}) custom-call(s32[1]{0:T(128)} %bitcast.refs_0_.w_ref, bf16[3,96,768]{2,1,0:T(8,128)(2,1)} %copy-done, bf16[3,96,768]{2,1,0:T(8,128)(2,1)} %copy-done.3, bf16[3,96,768]{2,1,0:T(8,128)(2,1)} %copy-done.1, ...), custom_call_target="tpu_custom_call" | custom-call | flops 756547584 | bytes 1179648 | tf_op jit(solution)/shard_map/attend2/pallas_call | solution.py:544
  124.5 6.9 %attend3.1 = (f32[416,768]{1,0:T(8,128)}, bf16[3,416,192]{2,1,0:T(8,128)(2,1)}, bf16[6,208,208]{2,1,0:T(8,128)(2,1)}, bf16[416,192]{1,0:T(8,128)(2,1)}) custom-call(s32[1]{0:T(128)} %bitcast.refs_0_.w_ref, bf16[3,96,768]{2,1,0:T(8,128)(2,1)} %copy-done, bf16[3,96,768]{2,1,0:T(8,128)(2,1)} %copy-done.3, bf16[3,96,768]{2,1,0:T(8,128)(2,1)} %copy-done.1, ...), custom_call_target="tpu_custom_call" | custom-call | flops 756547584 | bytes 1179648 | tf_op jit(solution)/shard_map/attend3/pallas_call | solution.py:544
  131.4 3.6 middle.1
  136.3 9.8 %mlp0.1 = (f32[416,768]{1,0:T(8,128)}, f32[416,768]{1,0:T(8,128)}, f32[1,768]{1,0:T(1,128)}, bf16[4,2,96,768]{3,2,1,0:T(8,128)(2,1)}, bf16[4,2,96,768]{3,2,1,0:T(8,128)(2,1)}) custom-call(s32[1]{0:T(128)} %bitcast.refs_0_.w_ref, bf16[768,768]{1,0:T(8,128)(2,1)} %refs_1_.1, bf16[768,768]{1,0:T(8,128)(2,1)} %refs_2_.1, ...), custom_call_target="tpu_custom_call" | custom-call | flops 2944401408 | bytes 1179648 | tf_op jit(solution)/shard_map/mlp0/pallas_call | solution.py:577
  149.5 10.8 %mlp1.1 = (f32[416,768]{1,0:T(8,128)}, f32[416,768]{1,0:T(8,128)}, f32[1,768]{1,0:T(1,128)}, bf16[4,2,96,768]{3,2,1,0:T(8,128)(2,1)}, bf16[4,2,96,768]{3,2,1,0:T(8,128)(2,1)}) custom-call(s32[1]{0:T(128)} %bitcast.refs_0_.w_ref, bf16[3,96,768]{2,1,0:T(8,128)(2,1)} %copy-done.10, bf16[3,96,768]{2,1,0:T(8,128)(2,1)} %copy-done.19, ...), custom_call_target="tpu_custom_call" | custom-call | flops 2944401408 | bytes 1179648 | tf_op jit(solution)/shard_map/mlp1/pallas_call | solution.py:577
  160.6 11.1 %mlp2.1 = (f32[416,768]{1,0:T(8,128)}, f32[416,768]{1,0:T(8,128)}, f32[1,768]{1,0:T(1,128)}, bf16[4,2,96,768]{3,2,1,0:T(8,128)(2,1)}, bf16[4,2,96,768]{3,2,1,0:T(8,128)(2,1)}) custom-call(s32[1]{0:T(128)} %bitcast.refs_0_.w_ref, bf16[3,96,768]{2,1,0:T(8,128)(2,1)} %copy-done.10, bf16[3,96,768]{2,1,0:T(8,128)(2,1)} %copy-done.19, ...), custom_call_target="tpu_custom_call" | custom-call | flops 2944401408 | bytes 1179648 | tf_op jit(solution)/shard_map/mlp2/pallas_call | solution.py:577
  171.7 10.7 %mlp3.1 = (f32[416,768]{1,0:T(8,128)}, f32[416,768]{1,0:T(8,128)}, f32[1,768]{1,0:T(1,128)}, bf16[4,2,96,768]{3,2,1,0:T(8,128)(2,1)}, bf16[4,2,96,768]{3,2,1,0:T(8,128)(2,1)}) custom-call(s32[1]{0:T(128)} %bitcast.refs_0_.w_ref, bf16[3,96,768]{2,1,0:T(8,128)(2,1)} %copy-done.10, bf16[3,96,768]{2,1,0:T(8,128)(2,1)} %copy-done.19, ...), custom_call_target="tpu_custom_call" | custom-call | flops 2944401408 | bytes 1179648 | tf_op jit(solution)/shard_map/mlp3/pallas_call | solution.py:577
  182.4 5.4 %turn.1 = (bf16[416,768]{1,0:T(8,128)(2,1)}, f32[416,768]{1,0:T(8,128)}, bf16[416,768]{1,0:T(8,128)(2,1)}, f32[8,768]{1,0:T(8,128)}) custom-call(f32[416,768]{1,0:T(8,128)} %get-tuple-element.92.mid_ref, f32[416,768]{1,0:T(8,128)} %get-tuple-element.101.out_ref, f32[416,768]{1,0:T(8,128)} %get-tuple-element.102.back_ref, bf16[416,768]{1,0:T(8,128)(2,1)} %bitcast.155, ...), custom_call_target="tpu_custom_call" | custom-call | tf_op jit(solution)/shard_map/turn/pallas_call | solution.py:597
  187.7 8.4 %attend_back1.1 = (f32[416,768]{1,0:T(8,128)}, f32[1,576]{1,0:T(1,128)}, f32[3,208,208]{2,1,0:T(8,128)}, bf16[4,1,96,768]{3,2,1,0:T(8,128)(2,1)}, bf16[4,1,96,768]{3,2,1,0:T(8,128)(2,1)}) custom-call(s32[1]{0:T(128)} %bitcast.refs_0_.w_ref, bf16[3,96,768]{2,1,0:T(8,128)(2,1)} %copy-done, bf16[3,96,768]{2,1,0:T(8,128)(2,1)} %copy-done.3, ...), custom_call_target="tpu_custom_call" | custom-call | flops 1513095168 | bytes 1179648 | tf_op jit(solution)/shard_map/attend_back1/pallas_call | solution.py:618
  196.2 9.1 %attend_back2.1 = (f32[416,768]{1,0:T(8,128)}, f32[1,576]{1,0:T(1,128)}, f32[3,208,208]{2,1,0:T(8,128)}, bf16[4,1,96,768]{3,2,1,0:T(8,128)(2,1)}, bf16[4,1,96,768]{3,2,1,0:T(8,128)(2,1)}) custom-call(s32[1]{0:T(128)} %bitcast.refs_0_.w_ref, bf16[3,96,768]{2,1,0:T(8,128)(2,1)} %copy-done, bf16[3,96,768]{2,1,0:T(8,128)(2,1)} %copy-done.3, ...), custom_call_target="tpu_custom_call" | custom-call | flops 1513095168 | bytes 1179648 | tf_op jit(solution)/shard_map/attend_back2/pallas_call | solution.py:618
  205.3 8.9 %attend_back3.1 = (f32[416,768]{1,0:T(8,128)}, f32[1,576]{1,0:T(1,128)}, f32[3,208,208]{2,1,0:T(8,128)}, bf16[4,1,96,768]{3,2,1,0:T(8,128)(2,1)}, bf16[4,1,96,768]{3,2,1,0:T(8,128)(2,1)}) custom-call(s32[1]{0:T(128)} %bitcast.refs_0_.w_ref, bf16[3,96,768]{2,1,0:T(8,128)(2,1)} %copy-done, bf16[3,96,768]{2,1,0:T(8,128)(2,1)} %copy-done.3, ...), custom_call_target="tpu_custom_call" | custom-call | flops 1513095168 | bytes 1179648 | tf_op jit(solution)/shard_map/attend_back3/pallas_call | solution.py:618
  214.1 8.9 %attend_back0.1 = (f32[416,768]{1,0:T(8,128)}, f32[1,576]{1,0:T(1,128)}, f32[3,208,208]{2,1,0:T(8,128)}, bf16[4,1,96,768]{3,2,1,0:T(8,128)(2,1)}, bf16[4,1,96,768]{3,2,1,0:T(8,128)(2,1)}) custom-call(s32[1]{0:T(128)} %bitcast.refs_0_.w_ref, bf16[768,768]{1,0:T(8,128)(2,1)} %pad_maximum_fusion.refs_1_, bf16[416,768]{1,0:T(8,128)(2,1)} %first.1.refs_2_.refs_11_, ...), custom_call_target="tpu_custom_call" | custom-call | flops 1513095168 | bytes 1179648 | tf_op jit(solution)/shard_map/attend_back0/pallas_call | solution.py:618
  223.0 14.2 %table.1 = f32[288,32]{1,0:T(8,128)} custom-call(s32[208,256]{1,0:T(8,128)} %pad.23.buckets_ref.refs_0_, f32[3,208,208]{2,1,0:T(8,128)} %get-tuple-element.127.refs_1_, f32[3,208,208]{2,1,0:T(8,128)} %get-tuple-element.128.refs_2_, f32[3,208,208]{2,1,0:T(8,128)} %get-tuple-element.129.refs_3_, f32[3,208,208]{2,1,0:T(8,128)} %get-tuple-element.130.refs_4_), custom_call_target="tpu_custom_call" | custom-call | flops 3189768192 | tf_op jit(solution)/shard_map/table/pallas_call | solution.py:647
  243.9 4.1 last.1
  264.3 3.8 collective-permute-done.40
  277.1 7.1 %collective-permute-done.46 = bf16[2,1,96,768]{3,2,1,0:T(8,128)(2,1)S(1)} collective-permute-done((bf16[2,1,96,768]{3,2,1,0:T(8,128)(2,1)S(1)}, bf16[2,1,96,768]{3,2,1,0:T(8,128)(2,1)S(1)}, u32[]{:S(2)}, u32[]{:S(2)}) %collective-permute-start.46) | collective-permute-done | bytes 294944 | tf_op jit(solution)/shard_map/ppermute | solution.py:409
  285.9 6.8 %collective-permute-done.53 = bf16[2,1,96,768]{3,2,1,0:T(8,128)(2,1)S(1)} collective-permute-done((bf16[2,1,96,768]{3,2,1,0:T(8,128)(2,1)S(1)}, bf16[2,1,96,768]{3,2,1,0:T(8,128)(2,1)S(1)}, u32[]{:S(2)}, u32[]{:S(2)}) %collective-permute-start.53) | collective-permute-done | bytes 294944 | tf_op jit(solution)/shard_map/ppermute | solution.py:409
  294.6 4.5 %collective-permute-done.50 = bf16[1,96,768]{2,1,0:T(8,128)(2,1)S(1)} collective-permute-done((bf16[1,96,768]{2,1,0:T(8,128)(2,1)S(1)}, bf16[1,96,768]{2,1,0:T(8,128)(2,1)S(1)}, u32[]{:S(2)}, u32[]{:S(2)}) %collective-permute-start.50) | collective-permute-done | bytes 147488 | tf_op jit(solution)/shard_map/ppermute | solution.py:409
  305.9 13.7 %collective-permute-done.69 = bf16[2,2,96,768]{3,2,1,0:T(8,128)(2,1)S(1)} collective-permute-done((bf16[2,2,96,768]{3,2,1,0:T(8,128)(2,1)S(1)}, bf16[2,2,96,768]{3,2,1,0:T(8,128)(2,1)S(1)}, u32[]{:S(2)}, u32[]{:S(2)}) %collective-permute-start.69) | collective-permute-done | bytes 589856 | tf_op jit(solution)/shard_map/ppermute | solution.py:409
  321.9 8.5 %collective-permute-done.76 = bf16[2,2,96,768]{3,2,1,0:T(8,128)(2,1)S(1)} collective-permute-done((bf16[2,2,96,768]{3,2,1,0:T(8,128)(2,1)S(1)}, bf16[2,2,96,768]{3,2,1,0:T(8,128)(2,1)S(1)}, u32[]{:S(2)}, u32[]{:S(2)}) %collective-permute-start.76) | collective-permute-done | bytes 589856 | tf_op jit(solution)/shard_map/ppermute | solution.py:409
  331.0 4.9 %collective-permute-done.80 = bf16[2,2,96,768]{3,2,1,0:T(8,128)(2,1)S(1)} collective-permute-done((bf16[2,2,96,768]{3,2,1,0:T(8,128)(2,1)S(1)}, bf16[2,2,96,768]{3,2,1,0:T(8,128)(2,1)S(1)}, u32[]{:S(2)}, u32[]{:S(2)}) %collective-permute-start.80) | collective-permute-done | bytes 589856 | tf_op jit(solution)/shard_map/ppermute | solution.py:409
  338.2 5.7 %collective-permute-done.77 = bf16[2,96,768]{2,1,0:T(8,128)(2,1)S(1)} collective-permute-done((bf16[2,96,768]{2,1,0:T(8,128)(2,1)S(1)}, bf16[2,96,768]{2,1,0:T(8,128)(2,1)S(1)}, u32[]{:S(2)}, u32[]{:S(2)}) %collective-permute-start.77) | collective-permute-done | bytes 294944 | tf_op jit(solution)/shard_map/ppermute | solution.py:409
  344.6 3.4 collective-permute-start.78
  351.5 4.2 %collective-permute-done.74 = bf16[2,96,768]{2,1,0:T(8,128)(2,1)S(1)} collective-permute-done((bf16[2,96,768]{2,1,0:T(8,128)(2,1)S(1)}, bf16[2,96,768]{2,1,0:T(8,128)(2,1)S(1)}, u32[]{:S(2)}, u32[]{:S(2)}) %collective-permute-start.74) | collective-permute-done | bytes 294944 | tf_op jit(solution)/shard_map/ppermute | solution.py:414
  355.7 8.2 %collective-permute-start.51 = (bf16[1,96,768]{2,1,0:T(8,128)(2,1)S(1)}, bf16[1,96,768]{2,1,0:T(8,128)(2,1)S(1)}, u32[]{:S(2)}, u32[]{:S(2)}) collective-permute-start(bf16[1,96,768]{2,1,0:T(8,128)(2,1)S(1)} %fusion.14), channel_id=1, source_target_pairs={{0,1},{1,2},{2,3},{3,0},{4,5},{5,6},{6,7},{7,4},{8,9},{9,10},{10,1... | collective-permute-start | bytes 442376 | tf_op jit(solution)/shard_map/ppermute | solution.py:414
  365.8 12.0 %collective-permute-start.59 = (bf16[1,96,768]{2,1,0:T(8,128)(2,1)S(1)}, bf16[1,96,768]{2,1,0:T(8,128)(2,1)S(1)}, u32[]{:S(2)}, u32[]{:S(2)}) collective-permute-start(bf16[1,96,768]{2,1,0:T(8,128)(2,1)S(1)} %fusion.12), channel_id=1, source_target_pairs={{0,3},{1,0},{2,1},{3,2},{4,7},{5,4},{6,5},{7,6},{8,11},{9,8},{10,9... | collective-permute-start | bytes 442376 | tf_op jit(solution)/shard_map/ppermute | solution.py:414
  386.3 3.7 collective-permute-done.61.refs_2_
  396.8 5.4 %collective-permute-done.89 = bf16[2,48,768]{2,1,0:T(8,128)(2,1)S(1)} collective-permute-done((bf16[2,48,768]{2,1,0:T(8,128)(2,1)S(1)}, bf16[2,48,768]{2,1,0:T(8,128)(2,1)S(1)}, u32[]{:S(2)}, u32[]{:S(2)}) %collective-permute-start.89) | collective-permute-done | bytes 147488 | tf_op jit(solution)/shard_map/ppermute | solution.py:409
  405.9 3.0 attend_final.1
  410.6 4.1 mlp_final.1
  (458 shorter events, 124.3 us)
Async XLA Ops:
  1.8 16.0 %collective-permute-start = (bf16[96,768]{1,0:T(8,128)(2,1)S(1)}, bf16[96,768]{1,0:T(8,128)(2,1)S(1)}, u32[]{:S(2)}, u32[]{:S(2)}) collective-permute-start(bf16[96,768]{1,0:T(8,128)(2,1)S(1)} %fusion.16), channel_id=1, source_target_pairs={{0,3},{1,0},{2,1},{3,2},{4,7},{5,4},{6,5},{7,6},{8,11},{9,8},{10,9... | collective-permute-start | bytes 442376 | tf_op jit(solution)/shard_map/ppermute | solution.py:414
  6.9 24.2 %collective-permute-start.1 = (bf16[96,768]{1,0:T(8,128)(2,1)S(1)}, bf16[96,768]{1,0:T(8,128)(2,1)S(1)}, u32[]{:S(2)}, u32[]{:S(2)}) collective-permute-start(bf16[96,768]{1,0:T(8,128)(2,1)S(1)} %fusion.16), channel_id=1, source_target_pairs={{0,2},{1,3},{2,0},{3,1},{4,6},{5,7},{6,4},{7,5},{8,10},{9,11},{10,... | collective-permute-start | bytes 442376 | tf_op jit(solution)/shard_map/ppermute | solution.py:414
  6.9 28.1 %collective-permute-start.2 = (bf16[96,768]{1,0:T(8,128)(2,1)S(1)}, bf16[96,768]{1,0:T(8,128)(2,1)S(1)}, u32[]{:S(2)}, u32[]{:S(2)}) collective-permute-start(bf16[96,768]{1,0:T(8,128)(2,1)S(1)} %fusion.16), channel_id=1, source_target_pairs={{0,1},{1,2},{2,3},{3,0},{4,5},{5,6},{6,7},{7,4},{8,9},{9,10},{10,1... | collective-permute-start | bytes 442376 | tf_op jit(solution)/shard_map/ppermute | solution.py:414
  9.5 25.5 %collective-permute-start.15 = (bf16[96,768]{1,0:T(8,128)(2,1)}, bf16[96,768]{1,0:T(8,128)(2,1)S(1)}, u32[]{:S(2)}, u32[]{:S(2)}) collective-permute-start(bf16[96,768]{1,0:T(8,128)(2,1)} %constant_dynamic-slice_fusion.1), channel_id=1, source_target_pairs={{0,3},{1,0},{2,1},{3,2},{4,7},{5,4},{6,5},{7,6},{8,11},{9,8},{10,9... | collective-permute-start | bytes 442376 | tf_op jit(solution)/shard_map/ppermute | solution.py:414
  12.3 23.8 %collective-permute-start.16 = (bf16[96,768]{1,0:T(8,128)(2,1)}, bf16[96,768]{1,0:T(8,128)(2,1)S(1)}, u32[]{:S(2)}, u32[]{:S(2)}) collective-permute-start(bf16[96,768]{1,0:T(8,128)(2,1)} %constant_dynamic-slice_fusion.1), channel_id=1, source_target_pairs={{0,2},{1,3},{2,0},{3,1},{4,6},{5,7},{6,4},{7,5},{8,10},{9,11},{10,... | collective-permute-start | bytes 442376 | tf_op jit(solution)/shard_map/ppermute | solution.py:414
  17.7 19.8 %collective-permute-start.17 = (bf16[96,768]{1,0:T(8,128)(2,1)}, bf16[96,768]{1,0:T(8,128)(2,1)S(1)}, u32[]{:S(2)}, u32[]{:S(2)}) collective-permute-start(bf16[96,768]{1,0:T(8,128)(2,1)} %constant_dynamic-slice_fusion.1), channel_id=1, source_target_pairs={{0,1},{1,2},{2,3},{3,0},{4,5},{5,6},{6,7},{7,4},{8,9},{9,10},{10,1... | collective-permute-start | bytes 442376 | tf_op jit(solution)/shard_map/ppermute | solution.py:414
  36.0 20.6 %collective-permute-start.4 = (bf16[3,96,768]{2,1,0:T(8,128)(2,1)S(1)}, bf16[3,96,768]{2,1,0:T(8,128)(2,1)S(1)}, u32[]{:S(2)}, u32[]{:S(2)}) collective-permute-start(bf16[3,96,768]{2,1,0:T(8,128)(2,1)S(1)} %pad_maximum_fusion.1.refs_1_), channel_id=1, source_target_pairs={{0,8},{4,12},{8,0},{12,4},{16,24},{20,28},{24,16},{28,20},{1,9},{5... | collective-permute-start | bytes 1327112 | tf_op jit(solution)/shard_map/ppermute | solution.py:409
  37.5 20.7 %collective-permute-start.6 = (bf16[3,96,768]{2,1,0:T(8,128)(2,1)S(1)}, bf16[3,96,768]{2,1,0:T(8,128)(2,1)S(1)}, u32[]{:S(2)}, u32[]{:S(2)}) collective-permute-start(bf16[3,96,768]{2,1,0:T(8,128)(2,1)S(1)} %pad_maximum_fusion.1.refs_1_), channel_id=1, source_target_pairs={{0,16},{4,20},{8,24},{12,28},{16,0},{20,4},{24,8},{28,12},{1,17},{... | collective-permute-start | bytes 1327112 | tf_op jit(solution)/shard_map/ppermute | solution.py:409
  39.1 20.6 %collective-permute-start.19 = (bf16[3,96,768]{2,1,0:T(8,128)(2,1)S(1)}, bf16[3,96,768]{2,1,0:T(8,128)(2,1)S(1)}, u32[]{:S(2)}, u32[]{:S(2)}) collective-permute-start(bf16[3,96,768]{2,1,0:T(8,128)(2,1)S(1)} %pad_maximum_fusion.2.refs_1_), channel_id=1, source_target_pairs={{0,8},{4,12},{8,0},{12,4},{16,24},{20,28},{24,16},{28,20},{1,9},{5... | collective-permute-start | bytes 1327112 | tf_op jit(solution)/shard_map/ppermute | solution.py:409
  39.8 10.8 %collective-permute-start.28 = (bf16[96,768]{1,0:T(8,128)(2,1)S(1)}, bf16[96,768]{1,0:T(8,128)(2,1)S(1)}, u32[]{:S(2)}, u32[]{:S(2)}) collective-permute-start(bf16[96,768]{1,0:T(8,128)(2,1)S(1)} %copy-done.55), channel_id=1, source_target_pairs={{0,2},{1,3},{2,0},{3,1},{4,6},{5,7},{6,4},{7,5},{8,10},{9,11},{10,... | collective-permute-start | bytes 442376 | tf_op jit(solution)/shard_map/ppermute | solution.py:414
  51.2 12.3 %collective-permute-start.21 = (bf16[3,96,768]{2,1,0:T(8,128)(2,1)S(1)}, bf16[3,96,768]{2,1,0:T(8,128)(2,1)S(1)}, u32[]{:S(2)}, u32[]{:S(2)}) collective-permute-start(bf16[3,96,768]{2,1,0:T(8,128)(2,1)S(1)} %pad_maximum_fusion.2.refs_1_), channel_id=1, source_target_pairs={{0,16},{4,20},{8,24},{12,28},{16,0},{20,4},{24,8},{28,12},{1,17},{... | collective-permute-start | bytes 1327112 | tf_op jit(solution)/shard_map/ppermute | solution.py:409
  56.7 13.2 %collective-permute-start.31 = (bf16[3,96,768]{2,1,0:T(8,128)(2,1)}, bf16[3,96,768]{2,1,0:T(8,128)(2,1)S(1)}, u32[]{:S(2)}, u32[]{:S(2)}) collective-permute-start(bf16[3,96,768]{2,1,0:T(8,128)(2,1)} %pad_maximum_fusion.3.refs_11_), channel_id=1, source_target_pairs={{0,8},{4,12},{8,0},{12,4},{16,24},{20,28},{24,16},{28,20},{1,9},{5... | collective-permute-start | bytes 1327112 | tf_op jit(solution)/shard_map/ppermute | solution.py:409
  58.2 14.7 %collective-permute-start.33 = (bf16[3,96,768]{2,1,0:T(8,128)(2,1)}, bf16[3,96,768]{2,1,0:T(8,128)(2,1)S(1)}, u32[]{:S(2)}, u32[]{:S(2)}) collective-permute-start(bf16[3,96,768]{2,1,0:T(8,128)(2,1)} %pad_maximum_fusion.3.refs_11_), channel_id=1, source_target_pairs={{0,16},{4,20},{8,24},{12,28},{16,0},{20,4},{24,8},{28,12},{1,17},{... | collective-permute-start | bytes 1327112 | tf_op jit(solution)/shard_map/ppermute | solution.py:409
  59.8 15.6 %collective-permute-start.18 = (bf16[3,96,768]{2,1,0:T(8,128)(2,1)S(1)}, bf16[3,96,768]{2,1,0:T(8,128)(2,1)S(1)}, u32[]{:S(2)}, u32[]{:S(2)}) collective-permute-start(bf16[3,96,768]{2,1,0:T(8,128)(2,1)S(1)} %pad_maximum_fusion.2.refs_1_), channel_id=1, source_target_pairs={{0,4},{4,0},{8,12},{12,8},{16,20},{20,16},{24,28},{28,24},{1,5},{5... | collective-permute-start | bytes 1327112 | tf_op jit(solution)/shard_map/ppermute | solution.py:409
  63.4 14.2 %collective-permute-start.8 = (bf16[3,48,768]{2,1,0:T(8,128)(2,1)S(1)}, bf16[3,48,768]{2,1,0:T(8,128)(2,1)S(1)}, u32[]{:S(2)}, u32[]{:S(2)}) collective-permute-start(bf16[3,48,768]{2,1,0:T(8,128)(2,1)S(1)} %slice.642), channel_id=1, source_target_pairs={{0,16},{4,20},{8,24},{12,28},{16,0},{20,4},{24,8},{28,12},{1,17},{... | collective-permute-start | bytes 663560 | tf_op jit(solution)/shard_map/ppermute | solution.py:409
  64.3 13.3 %collective-permute-start.9 = (bf16[3,48,768]{2,1,0:T(8,128)(2,1)S(1)}, bf16[3,48,768]{2,1,0:T(8,128)(2,1)S(1)}, u32[]{:S(2)}, u32[]{:S(2)}) collective-permute-start(bf16[3,48,768]{2,1,0:T(8,128)(2,1)S(1)} %slice.643), channel_id=1, source_target_pairs={{0,8},{4,12},{8,0},{12,4},{16,24},{20,28},{24,16},{28,20},{1,9},{5... | collective-permute-start | bytes 663560 | tf_op jit(solution)/shard_map/ppermute | solution.py:409
  69.9 11.5 %collective-permute-start.23 = (bf16[3,48,768]{2,1,0:T(8,128)(2,1)S(1)}, bf16[3,48,768]{2,1,0:T(8,128)(2,1)}, u32[]{:S(2)}, u32[]{:S(2)}) collective-permute-start(bf16[3,48,768]{2,1,0:T(8,128)(2,1)S(1)} %slice.653), channel_id=1, source_target_pairs={{0,16},{4,20},{8,24},{12,28},{16,0},{20,4},{24,8},{28,12},{1,17},{... | collective-permute-start | bytes 663560 | tf_op jit(solution)/shard_map/ppermute | solution.py:409
  75.4 10.1 %collective-permute-start.5 = (bf16[3,96,768]{2,1,0:T(8,128)(2,1)S(1)}, bf16[3,96,768]{2,1,0:T(8,128)(2,1)S(1)}, u32[]{:S(2)}, u32[]{:S(2)}) collective-permute-start(bf16[3,96,768]{2,1,0:T(8,128)(2,1)S(1)} %collective-permute-done.4.refs_3_), channel_id=1, source_target_pairs={{0,4},{4,0},{8,12},{12,8},{16,20},{20,16},{24,28},{28,24},{1,5},{5... | collective-permute-start | bytes 1327112 | tf_op jit(solution)/shard_map/ppermute | solution.py:409
  77.7 57.3 %collective-permute-start.30 = (bf16[3,96,768]{2,1,0:T(8,128)(2,1)}, bf16[3,96,768]{2,1,0:T(8,128)(2,1)S(1)}, u32[]{:S(2)}, u32[]{:S(2)}) collective-permute-start(bf16[3,96,768]{2,1,0:T(8,128)(2,1)} %pad_maximum_fusion.3.refs_11_), channel_id=1, source_target_pairs={{0,4},{4,0},{8,12},{12,8},{16,20},{20,16},{24,28},{28,24},{1,5},{5... | collective-permute-start | bytes 1327112 | tf_op jit(solution)/shard_map/ppermute | solution.py:409
  82.9 52.3 %collective-permute-start.35 = (bf16[3,48,768]{2,1,0:T(8,128)(2,1)S(1)}, bf16[3,48,768]{2,1,0:T(8,128)(2,1)}, u32[]{:S(2)}, u32[]{:S(2)}) collective-permute-start(bf16[3,48,768]{2,1,0:T(8,128)(2,1)S(1)} %slice.655), channel_id=1, source_target_pairs={{0,16},{4,20},{8,24},{12,28},{16,0},{20,4},{24,8},{28,12},{1,17},{... | collective-permute-start | bytes 663560 | tf_op jit(solution)/shard_map/ppermute | solution.py:409
  84.0 51.5 %collective-permute-start.36 = (bf16[3,48,768]{2,1,0:T(8,128)(2,1)S(1)}, bf16[3,48,768]{2,1,0:T(8,128)(2,1)}, u32[]{:S(2)}, u32[]{:S(2)}) collective-permute-start(bf16[3,48,768]{2,1,0:T(8,128)(2,1)S(1)} %slice.656), channel_id=1, source_target_pairs={{0,8},{4,12},{8,0},{12,4},{16,24},{20,28},{24,16},{28,20},{1,9},{5... | collective-permute-start | bytes 663560 | tf_op jit(solution)/shard_map/ppermute | solution.py:409
  85.5 50.2 %collective-permute-start.25 = (bf16[3,48,768]{2,1,0:T(8,128)(2,1)}, bf16[3,48,768]{2,1,0:T(8,128)(2,1)S(1)}, u32[]{:S(2)}, u32[]{:S(2)}) collective-permute-start(bf16[3,48,768]{2,1,0:T(8,128)(2,1)} %collective-permute-done.23.refs_7_), channel_id=1, source_target_pairs={{0,4},{4,0},{8,12},{12,8},{16,20},{20,16},{24,28},{28,24},{1,5},{5... | collective-permute-start | bytes 663560 | tf_op jit(solution)/shard_map/ppermute | solution.py:409
  85.5 50.7 %collective-permute-start.26 = (bf16[3,48,768]{2,1,0:T(8,128)(2,1)}, bf16[3,48,768]{2,1,0:T(8,128)(2,1)S(1)}, u32[]{:S(2)}, u32[]{:S(2)}) collective-permute-start(bf16[3,48,768]{2,1,0:T(8,128)(2,1)} %collective-permute-done.24.refs_8_), channel_id=1, source_target_pairs={{0,4},{4,0},{8,12},{12,8},{16,20},{20,16},{24,28},{28,24},{1,5},{5... | collective-permute-start | bytes 663560 | tf_op jit(solution)/shard_map/ppermute | solution.py:409
  135.0 13.3 %collective-permute-start.20 = (bf16[3,96,768]{2,1,0:T(8,128)(2,1)S(1)}, bf16[3,96,768]{2,1,0:T(8,128)(2,1)S(1)}, u32[]{:S(2)}, u32[]{:S(2)}) collective-permute-start(bf16[3,96,768]{2,1,0:T(8,128)(2,1)S(1)} %copy-done.12), channel_id=1, source_target_pairs={{0,4},{4,0},{8,12},{12,8},{16,20},{20,16},{24,28},{28,24},{1,5},{5... | collective-permute-start | bytes 1327112 | tf_op jit(solution)/shard_map/ppermute | solution.py:409
  135.2 13.1 %collective-permute-start.22 = (bf16[3,96,768]{2,1,0:T(8,128)(2,1)S(1)}, bf16[3,96,768]{2,1,0:T(8,128)(2,1)S(1)}, u32[]{:S(2)}, u32[]{:S(2)}) collective-permute-start(bf16[3,96,768]{2,1,0:T(8,128)(2,1)S(1)} %copy-done.14), channel_id=1, source_target_pairs={{0,4},{4,0},{8,12},{12,8},{16,20},{20,16},{24,28},{28,24},{1,5},{5... | collective-permute-start | bytes 1327112 | tf_op jit(solution)/shard_map/ppermute | solution.py:409
  135.6 12.7 %collective-permute-start.32 = (bf16[3,96,768]{2,1,0:T(8,128)(2,1)S(1)}, bf16[3,96,768]{2,1,0:T(8,128)(2,1)S(1)}, u32[]{:S(2)}, u32[]{:S(2)}) collective-permute-start(bf16[3,96,768]{2,1,0:T(8,128)(2,1)S(1)} %copy-done.16), channel_id=1, source_target_pairs={{0,4},{4,0},{8,12},{12,8},{16,20},{20,16},{24,28},{28,24},{1,5},{5... | collective-permute-start | bytes 1327112 | tf_op jit(solution)/shard_map/ppermute | solution.py:409
  135.7 12.7 %collective-permute-start.34 = (bf16[3,96,768]{2,1,0:T(8,128)(2,1)S(1)}, bf16[3,96,768]{2,1,0:T(8,128)(2,1)S(1)}, u32[]{:S(2)}, u32[]{:S(2)}) collective-permute-start(bf16[3,96,768]{2,1,0:T(8,128)(2,1)S(1)} %copy-done.18), channel_id=1, source_target_pairs={{0,4},{4,0},{8,12},{12,8},{16,20},{20,16},{24,28},{28,24},{1,5},{5... | collective-permute-start | bytes 1327112 | tf_op jit(solution)/shard_map/ppermute | solution.py:409
  148.0 152.2 %collective-permute-start.68 = (bf16[4,2,96,768]{3,2,1,0:T(8,128)(2,1)}, bf16[4,2,96,768]{3,2,1,0:T(8,128)(2,1)S(1)}, u32[]{:S(2)}, u32[]{:S(2)}) collective-permute-start(bf16[4,2,96,768]{3,2,1,0:T(8,128)(2,1)} %get-tuple-element.148), channel_id=1, source_target_pairs={{0,4},{4,0},{8,12},{12,8},{16,20},{20,16},{24,28},{28,24},{1,5},{5... | collective-permute-start | bytes 3538952 | tf_op jit(solution)/shard_map/ppermute | solution.py:409
  160.3 140.8 %collective-permute-start.71 = (bf16[4,2,96,768]{3,2,1,0:T(8,128)(2,1)}, bf16[4,2,96,768]{3,2,1,0:T(8,128)(2,1)S(1)}, u32[]{:S(2)}, u32[]{:S(2)}) collective-permute-start(bf16[4,2,96,768]{3,2,1,0:T(8,128)(2,1)} %get-tuple-element.150), channel_id=1, source_target_pairs={{0,4},{4,0},{8,12},{12,8},{16,20},{20,16},{24,28},{28,24},{1,5},{5... | collective-permute-start | bytes 3538952 | tf_op jit(solution)/shard_map/ppermute | solution.py:409
  264.1 10.8 %collective-permute-start.48 = (bf16[4,1,96,768]{3,2,1,0:T(8,128)(2,1)S(1)}, bf16[4,1,96,768]{3,2,1,0:T(8,128)(2,1)S(1)}, u32[]{:S(2)}, u32[]{:S(2)}) collective-permute-start(bf16[4,1,96,768]{3,2,1,0:T(8,128)(2,1)S(1)} %copy-done.78), channel_id=1, source_target_pairs={{0,4},{4,0},{8,12},{12,8},{16,20},{20,16},{24,28},{28,24},{1,5},{5... | collective-permute-start | bytes 1769480 | tf_op jit(solution)/shard_map/ppermute | solution.py:409
  274.7 28.1 %collective-permute-start.75 = (bf16[4,2,96,768]{3,2,1,0:T(8,128)(2,1)S(1)}, bf16[4,2,96,768]{3,2,1,0:T(8,128)(2,1)S(1)}, u32[]{:S(2)}, u32[]{:S(2)}) collective-permute-start(bf16[4,2,96,768]{3,2,1,0:T(8,128)(2,1)S(1)} %copy-done.77), channel_id=1, source_target_pairs={{0,4},{4,0},{8,12},{12,8},{16,20},{20,16},{24,28},{28,24},{1,5},{5... | collective-permute-start | bytes 3538952 | tf_op jit(solution)/shard_map/ppermute | solution.py:409
  292.7 11.6 %collective-permute-start.79 = (bf16[4,2,96,768]{3,2,1,0:T(8,128)(2,1)S(1)}, bf16[4,2,96,768]{3,2,1,0:T(8,128)(2,1)S(1)}, u32[]{:S(2)}, u32[]{:S(2)}) collective-permute-start(bf16[4,2,96,768]{3,2,1,0:T(8,128)(2,1)S(1)} %copy-done.76), channel_id=1, source_target_pairs={{0,4},{4,0},{8,12},{12,8},{16,20},{20,16},{24,28},{28,24},{1,5},{5... | collective-permute-start | bytes 3538952 | tf_op jit(solution)/shard_map/ppermute | solution.py:409
  299.1 49.1 %collective-permute-start.54 = (bf16[1,96,768]{2,1,0:T(8,128)(2,1)S(1)}, bf16[1,96,768]{2,1,0:T(8,128)(2,1)S(1)}, u32[]{:S(2)}, u32[]{:S(2)}) collective-permute-start(bf16[1,96,768]{2,1,0:T(8,128)(2,1)S(1)} %fusion.22), channel_id=1, source_target_pairs={{0,16},{4,20},{8,24},{12,28},{16,0},{20,4},{24,8},{28,12},{1,17},{... | collective-permute-start | bytes 442376 | tf_op jit(solution)/shard_map/ppermute | solution.py:409
  300.1 48.2 %collective-permute-start.58 = (bf16[1,96,768]{2,1,0:T(8,128)(2,1)S(1)}, bf16[1,96,768]{2,1,0:T(8,128)(2,1)S(1)}, u32[]{:S(2)}, u32[]{:S(2)}) collective-permute-start(bf16[1,96,768]{2,1,0:T(8,128)(2,1)S(1)} %fusion.24), channel_id=1, source_target_pairs={{0,8},{4,12},{8,0},{12,4},{16,24},{20,28},{24,16},{28,20},{1,9},{5... | collective-permute-start | bytes 442376 | tf_op jit(solution)/shard_map/ppermute | solution.py:409
  301.1 18.6 %collective-permute-start.69 = (bf16[2,2,96,768]{3,2,1,0:T(8,128)(2,1)S(1)}, bf16[2,2,96,768]{3,2,1,0:T(8,128)(2,1)S(1)}, u32[]{:S(2)}, u32[]{:S(2)}) collective-permute-start(bf16[2,2,96,768]{3,2,1,0:T(8,128)(2,1)S(1)} %add_convert_fusion.6), channel_id=1, source_target_pairs={{0,8},{4,12},{8,0},{12,4},{16,24},{20,28},{24,16},{28,20},{1,9},{5... | collective-permute-start | bytes 1769480 | tf_op jit(solution)/shard_map/ppermute | solution.py:409
  302.8 17.9 %collective-permute-start.72 = (bf16[2,2,96,768]{3,2,1,0:T(8,128)(2,1)S(1)}, bf16[2,2,96,768]{3,2,1,0:T(8,128)(2,1)S(1)}, u32[]{:S(2)}, u32[]{:S(2)}) collective-permute-start(bf16[2,2,96,768]{3,2,1,0:T(8,128)(2,1)S(1)} %get-tuple-element.158), channel_id=1, source_target_pairs={{0,16},{4,20},{8,24},{12,28},{16,0},{20,4},{24,8},{28,12},{1,17},{... | collective-permute-start | bytes 1769480 | tf_op jit(solution)/shard_map/ppermute | solution.py:409
  304.4 26.0 %collective-permute-start.76 = (bf16[2,2,96,768]{3,2,1,0:T(8,128)(2,1)S(1)}, bf16[2,2,96,768]{3,2,1,0:T(8,128)(2,1)S(1)}, u32[]{:S(2)}, u32[]{:S(2)}) collective-permute-start(bf16[2,2,96,768]{3,2,1,0:T(8,128)(2,1)S(1)} %add_convert_fusion.2), channel_id=1, source_target_pairs={{0,8},{4,12},{8,0},{12,4},{16,24},{20,28},{24,16},{28,20},{1,9},{5... | collective-permute-start | bytes 1769480 | tf_op jit(solution)/shard_map/ppermute | solution.py:409
  319.6 16.3 %collective-permute-start.80 = (bf16[2,2,96,768]{3,2,1,0:T(8,128)(2,1)S(1)}, bf16[2,2,96,768]{3,2,1,0:T(8,128)(2,1)S(1)}, u32[]{:S(2)}, u32[]{:S(2)}) collective-permute-start(bf16[2,2,96,768]{3,2,1,0:T(8,128)(2,1)S(1)} %get-tuple-element.160), channel_id=1, source_target_pairs={{0,16},{4,20},{8,24},{12,28},{16,0},{20,4},{24,8},{28,12},{1,17},{... | collective-permute-start | bytes 1769480 | tf_op jit(solution)/shard_map/ppermute | solution.py:409
  320.8 29.7 %collective-permute-start.70 = (bf16[2,96,768]{2,1,0:T(8,128)(2,1)S(1)}, bf16[2,96,768]{2,1,0:T(8,128)(2,1)S(1)}, u32[]{:S(2)}, u32[]{:S(2)}) collective-permute-start(bf16[2,96,768]{2,1,0:T(8,128)(2,1)S(1)} %fusion.5), channel_id=1, source_target_pairs={{0,16},{4,20},{8,24},{12,28},{16,0},{20,4},{24,8},{28,12},{1,17},{... | collective-permute-start | bytes 884744 | tf_op jit(solution)/shard_map/ppermute | solution.py:409
  343.9 11.8 %collective-permute-start.74 = (bf16[2,96,768]{2,1,0:T(8,128)(2,1)S(1)}, bf16[2,96,768]{2,1,0:T(8,128)(2,1)S(1)}, u32[]{:S(2)}, u32[]{:S(2)}) collective-permute-start(bf16[2,96,768]{2,1,0:T(8,128)(2,1)S(1)} %fusion.2), channel_id=1, source_target_pairs={{0,1},{1,2},{2,3},{3,0},{4,5},{5,6},{6,7},{7,4},{8,9},{9,10},{10,1... | collective-permute-start | bytes 884744 | tf_op jit(solution)/shard_map/ppermute | solution.py:414
  344.6 20.3 %collective-permute-start.78 = (bf16[2,96,768]{2,1,0:T(8,128)(2,1)S(1)}, bf16[2,96,768]{2,1,0:T(8,128)(2,1)S(1)}, u32[]{:S(2)}, u32[]{:S(2)}) collective-permute-start(bf16[2,96,768]{2,1,0:T(8,128)(2,1)S(1)} %fusion.1), channel_id=1, source_target_pairs={{0,2},{1,3},{2,0},{3,1},{4,6},{5,7},{6,4},{7,5},{8,10},{9,11},{10,... | collective-permute-start | bytes 884744 | tf_op jit(solution)/shard_map/ppermute | solution.py:414
  348.2 17.6 %collective-permute-start.82 = (bf16[2,96,768]{2,1,0:T(8,128)(2,1)S(1)}, bf16[2,96,768]{2,1,0:T(8,128)(2,1)S(1)}, u32[]{:S(2)}, u32[]{:S(2)}) collective-permute-start(bf16[2,96,768]{2,1,0:T(8,128)(2,1)S(1)} %fusion), channel_id=1, source_target_pairs={{0,3},{1,0},{2,1},{3,2},{4,7},{5,4},{6,5},{7,6},{8,11},{9,8},{10,9... | collective-permute-start | bytes 884744 | tf_op jit(solution)/shard_map/ppermute | solution.py:414
  348.4 35.1 %collective-permute-start.42 = (f32[81,128]{1,0:T(8,128)S(1)}, f32[81,128]{1,0:T(8,128)S(1)}, u32[]{:S(2)}, u32[]{:S(2)}) collective-permute-start(f32[81,128]{1,0:T(8,128)S(1)} %get-tuple-element.216), channel_id=1, source_target_pairs={{0,1},{1,2},{2,3},{3,0},{4,5},{5,6},{6,7},{7,4},{8,9},{9,10},{10,1... | collective-permute-start | bytes 124424 | tf_op jit(solution)/shard_map/ppermute | solution.py:414
  350.5 27.5 %collective-permute-start.47 = (bf16[1,96,768]{2,1,0:T(8,128)(2,1)S(1)}, bf16[1,96,768]{2,1,0:T(8,128)(2,1)S(1)}, u32[]{:S(2)}, u32[]{:S(2)}) collective-permute-start(bf16[1,96,768]{2,1,0:T(8,128)(2,1)S(1)} %fusion.18), channel_id=1, source_target_pairs={{0,16},{4,20},{8,24},{12,28},{16,0},{20,4},{24,8},{28,12},{1,17},{... | collective-permute-start | bytes 442376 | tf_op jit(solution)/shard_map/ppermute | solution.py:409
  355.7 24.4 %collective-permute-start.51 = (bf16[1,96,768]{2,1,0:T(8,128)(2,1)S(1)}, bf16[1,96,768]{2,1,0:T(8,128)(2,1)S(1)}, u32[]{:S(2)}, u32[]{:S(2)}) collective-permute-start(bf16[1,96,768]{2,1,0:T(8,128)(2,1)S(1)} %fusion.14), channel_id=1, source_target_pairs={{0,1},{1,2},{2,3},{3,0},{4,5},{5,6},{6,7},{7,4},{8,9},{9,10},{10,1... | collective-permute-start | bytes 442376 | tf_op jit(solution)/shard_map/ppermute | solution.py:414
  364.9 16.3 %collective-permute-start.55 = (bf16[1,96,768]{2,1,0:T(8,128)(2,1)S(1)}, bf16[1,96,768]{2,1,0:T(8,128)(2,1)S(1)}, u32[]{:S(2)}, u32[]{:S(2)}) collective-permute-start(bf16[1,96,768]{2,1,0:T(8,128)(2,1)S(1)} %fusion.13), channel_id=1, source_target_pairs={{0,2},{1,3},{2,0},{3,1},{4,6},{5,7},{6,4},{7,5},{8,10},{9,11},{10,... | collective-permute-start | bytes 442376 | tf_op jit(solution)/shard_map/ppermute | solution.py:414
  365.8 15.8 %collective-permute-start.59 = (bf16[1,96,768]{2,1,0:T(8,128)(2,1)S(1)}, bf16[1,96,768]{2,1,0:T(8,128)(2,1)S(1)}, u32[]{:S(2)}, u32[]{:S(2)}) collective-permute-start(bf16[1,96,768]{2,1,0:T(8,128)(2,1)S(1)} %fusion.12), channel_id=1, source_target_pairs={{0,3},{1,0},{2,1},{3,2},{4,7},{5,4},{6,5},{7,6},{8,11},{9,8},{10,9... | collective-permute-start | bytes 442376 | tf_op jit(solution)/shard_map/ppermute | solution.py:414
  383.5 12.4 %collective-permute-start.86 = (bf16[2,96,768]{2,1,0:T(8,128)(2,1)S(1)}, bf16[2,96,768]{2,1,0:T(8,128)(2,1)S(1)}, u32[]{:S(2)}, u32[]{:S(2)}) collective-permute-start(bf16[2,96,768]{2,1,0:T(8,128)(2,1)S(1)} %add_convert_fusion.8.refs_0_), channel_id=1, source_target_pairs={{0,16},{4,20},{8,24},{12,28},{16,0},{20,4},{24,8},{28,12},{1,17},{... | collective-permute-start | bytes 884744 | tf_op jit(solution)/shard_map/ppermute | solution.py:409
  (125 other events, 874.6 us)
